TPU v7x, 256 devices: a whole 4x4x8 slice. The times are simulated.
256 devices in a mesh: dp: 16 (over y, z_lo, core), ctx: 16 (over x, z_hi).
Axes of the slice: x: 4, y: 4, z: 8 (z_hi: 4, z_lo: 2; z = z_hi * 2 + z_lo), core: 2. Of those that a mesh axis runs over, the one named last changes fastest.
Arguments:
- layer_input: bfloat16 [32768, 8192], P(('dp', 'ctx')), may hold values from -24 to 24
- queries: bfloat16 [32768, 4096], P(('dp', 'ctx')), may hold values from -8 to 8
- layer_keys: bfloat16 [32768, 512], P(('dp', 'ctx')), may hold values from -8 to 8
- layer_values: bfloat16 [32768, 512], P(('dp', 'ctx')), may hold values from -6 to 6
- output_grad: bfloat16 [32768, 4096], P(('dp', 'ctx')), may hold values from -6 to 6
- segment_ids: int32 [16, 2048], P('dp'), may hold values from 0 to 7, never falling along the last dimension, each value on 1 to 512 neighbouring positions
- first_moment: float32 [8192, 512], P(('dp', 'ctx')), may hold values from -112 to 112
- second_moment: float32 [8192, 512], P(('dp', 'ctx')), may hold values from 16.384 to 163.84
Outputs:
- attention: bfloat16 [32768, 4096], P(('dp', 'ctx'))
- query_grad: bfloat16 [32768, 4096], P(('dp', 'ctx'))
- key_grad: bfloat16 [32768, 512], P(('dp', 'ctx'))
- projection_update: bfloat16 [8192, 512], P('dp')
Inputs may be any that keep to these rules, and one draw needn't show every extreme that they name: `segment_ids`: within each window the ids never fall; each rollout covers 1 to 512 positions, one exactly 512.
All inputs are finite; a program needn't handle non-finite values.
Results may differ from a plain program's by a relative error of at most 0.015.
Values may be sent and summed in bfloat16 or wider, within the bound.
A program may use at most 128 MiB of HBM per device.

v0:
```python
import jax
import jax.numpy as jnp
from jax import lax
from jax.sharding import PartitionSpec as P

HQ = 32
HK = 4
HD = 128


first_fix = 1.0 - 0.9**8
second_fix = 1.0 - 0.999**8


def attend(q_heads, grad_heads, k_head, v_head, segments, per_dev):
    length = k_head.shape[0]
    head_size = k_head.shape[1]
    block_len = min(512, length)
    block_count = length // block_len
    scaling = head_size ** (-0.5)
    q_three = q_heads.reshape(length, per_dev, head_size)
    g_three = grad_heads.reshape(length, per_dev, head_size)

    def scores(q_block, k_block):
        q_rows = lax.dynamic_slice_in_dim(q_three, q_block * block_len, block_len, 0)
        k_rows = lax.dynamic_slice_in_dim(k_head, k_block * block_len, block_len, 0)
        raw = (
            jnp.einsum("qhd,kd->hqk", q_rows, k_rows, preferred_element_type=jnp.float32) * scaling
        )
        row_pos = q_block * block_len + lax.iota(jnp.int32, block_len)
        col_pos = k_block * block_len + lax.iota(jnp.int32, block_len)
        seg_rows = lax.dynamic_slice_in_dim(segments, q_block * block_len, block_len, 0)
        seg_cols = lax.dynamic_slice_in_dim(segments, k_block * block_len, block_len, 0)
        allowed = (col_pos[None, :] <= row_pos[:, None]) & (seg_rows[:, None] == seg_cols[None, :])
        return (jnp.where(allowed[None], raw, -1e30), allowed)

    def row_stats(q_block, lse_all):

        def row_advance(k_block, carry):
            row_top, row_total = carry
            masked, allowed = scores(q_block, k_block)
            new_top = jnp.maximum(row_top, jnp.max(masked, axis=2))
            shifted = jnp.where(allowed[None], jnp.exp(masked - new_top[:, :, None]), 0.0)
            row_total = row_total * jnp.exp(row_top - new_top) + jnp.sum(shifted, axis=2)
            return (new_top, row_total)

        start = (
            jnp.full((per_dev, block_len), -1e30, jnp.float32),
            jnp.zeros((per_dev, block_len), jnp.float32),
        )
        row_top, row_total = lax.fori_loop(0, q_block + 1, row_advance, start)
        return lax.dynamic_update_slice_in_dim(
            lse_all, row_top + jnp.log(row_total), q_block * block_len, 1
        )

    log_total = lax.fori_loop(0, block_count, row_stats, jnp.zeros((per_dev, length), jnp.float32))

    def weights_for(q_block, k_block):
        masked, allowed = scores(q_block, k_block)
        lse_rows = lax.dynamic_slice_in_dim(log_total, q_block * block_len, block_len, 1)
        return jnp.where(allowed[None], jnp.exp(masked - lse_rows[:, :, None]), 0.0)

    def out_block(q_block, out_all):

        def out_advance(k_block, accum):
            probs_low = weights_for(q_block, k_block).astype(jnp.bfloat16)
            v_rows = lax.dynamic_slice_in_dim(v_head, k_block * block_len, block_len, 0)
            return accum + jnp.einsum(
                "hqk,kd->qhd", probs_low, v_rows, preferred_element_type=jnp.float32
            )

        accum = lax.fori_loop(
            0, q_block + 1, out_advance, jnp.zeros((block_len, per_dev, head_size), jnp.float32)
        )
        return lax.dynamic_update_slice_in_dim(
            out_all, accum.astype(jnp.bfloat16), q_block * block_len, 0
        )

    out_three = lax.fori_loop(
        0, block_count, out_block, jnp.zeros((length, per_dev, head_size), jnp.bfloat16)
    )
    delta = jnp.sum(g_three.astype(jnp.float32) * out_three.astype(jnp.float32), axis=2).T

    def key_block(k_block, carry):
        dq_all, dk_all, dv_all = carry
        k_rows = lax.dynamic_slice_in_dim(k_head, k_block * block_len, block_len, 0)
        v_rows = lax.dynamic_slice_in_dim(v_head, k_block * block_len, block_len, 0)

        def key_advance(q_block, inner):
            dq_inner, dk_accum, dv_accum = inner
            probs = weights_for(q_block, k_block)
            probs_low = probs.astype(jnp.bfloat16)
            q_rows = lax.dynamic_slice_in_dim(q_three, q_block * block_len, block_len, 0)
            g_rows = lax.dynamic_slice_in_dim(g_three, q_block * block_len, block_len, 0)
            dprobs = jnp.einsum("qhd,kd->hqk", g_rows, v_rows, preferred_element_type=jnp.float32)
            delta_rows = lax.dynamic_slice_in_dim(delta, q_block * block_len, block_len, 1)
            dscores = (probs * (dprobs - delta_rows[:, :, None])).astype(jnp.bfloat16)
            dq_part = (
                jnp.einsum("hqk,kd->qhd", dscores, k_rows, preferred_element_type=jnp.float32)
                * scaling
            )
            old_rows = lax.dynamic_slice_in_dim(dq_inner, q_block * block_len, block_len, 0)
            dq_inner = lax.dynamic_update_slice_in_dim(
                dq_inner, old_rows + dq_part, q_block * block_len, 0
            )
            dk_accum = dk_accum + jnp.einsum(
                "hqk,qhd->kd", dscores, q_rows, preferred_element_type=jnp.float32
            )
            dv_accum = dv_accum + jnp.einsum(
                "hqk,qhd->kd", probs_low, g_rows, preferred_element_type=jnp.float32
            )
            return (dq_inner, dk_accum, dv_accum)

        empty = jnp.zeros((block_len, head_size), jnp.float32)
        dq_all, dk_accum, dv_accum = lax.fori_loop(
            k_block, block_count, key_advance, (dq_all, empty, empty)
        )
        dk_all = lax.dynamic_update_slice_in_dim(
            dk_all, (dk_accum * scaling).astype(jnp.bfloat16), k_block * block_len, 0
        )
        dv_all = lax.dynamic_update_slice_in_dim(
            dv_all, dv_accum.astype(jnp.bfloat16), k_block * block_len, 0
        )
        return (dq_all, dk_all, dv_all)

    start = (
        jnp.zeros((length, per_dev, head_size), jnp.float32),
        jnp.zeros((length, head_size), jnp.bfloat16),
        jnp.zeros((length, head_size), jnp.bfloat16),
    )
    dq_all, dk_all, dv_all = lax.fori_loop(0, block_count, key_block, start)
    out_flat = out_three.reshape(length, per_dev * head_size)
    dq_flat = dq_all.astype(jnp.bfloat16).reshape(length, per_dev * head_size)
    return (out_flat, dq_flat, dk_all, dv_all)


def body(
    layer_input,
    queries,
    layer_keys,
    layer_values,
    output_grad,
    segment_ids,
    first_moment,
    second_moment,
):
    tok_rows = queries.shape[0]
    ctx_size = lax.axis_size("ctx")
    per_dev = HQ // ctx_size
    repeats = ctx_size // HK
    q_heads, grad_heads = (
        lax.all_to_all(queries, "ctx", split_axis=1, concat_axis=0, tiled=True),
        lax.all_to_all(output_grad, "ctx", split_axis=1, concat_axis=0, tiled=True),
    )
    k_whole, v_whole = (
        lax.all_gather(layer_keys, "ctx", axis=0, tiled=True),
        lax.all_gather(layer_values, "ctx", axis=0, tiled=True),
    )
    first_col = lax.axis_index("ctx") // repeats * HD
    k_head = lax.dynamic_slice_in_dim(k_whole, first_col, HD, 1)
    v_head = lax.dynamic_slice_in_dim(v_whole, first_col, HD, 1)
    out_heads, dq_heads, dk_part, dv_part = attend(
        q_heads, grad_heads, k_head, v_head, segment_ids[0], per_dev
    )
    attention, query_grad, dk_blocks, dv_blocks = (
        lax.all_to_all(out_heads, "ctx", split_axis=0, concat_axis=1, tiled=True),
        lax.all_to_all(dq_heads, "ctx", split_axis=0, concat_axis=1, tiled=True),
        lax.all_to_all(dk_part, "ctx", split_axis=0, concat_axis=1, tiled=True),
        lax.all_to_all(dv_part, "ctx", split_axis=0, concat_axis=1, tiled=True),
    )
    key_grad = jnp.sum(dk_blocks.reshape(tok_rows, HK, repeats, HD).astype(jnp.float32), axis=2)
    key_grad = key_grad.astype(jnp.bfloat16).reshape(tok_rows, HK * HD)
    value_grad = jnp.sum(dv_blocks.reshape(tok_rows, HK, repeats, HD).astype(jnp.float32), axis=2)
    value_grad = value_grad.astype(jnp.bfloat16).reshape(tok_rows, HK * HD)
    gradient = lax.psum_scatter(
        lax.dot_general(
            layer_input, value_grad, (((0,), (0,)), ((), ())), preferred_element_type=jnp.float32
        ),
        ("dp", "ctx"),
        scatter_dimension=0,
        tiled=True,
    )
    new_first = 0.9 * first_moment + 0.1 * gradient
    new_second = 0.999 * second_moment + 0.001 * gradient * gradient
    update = (new_first / first_fix / (jnp.sqrt(new_second / second_fix) + 1e-08)).astype(
        jnp.bfloat16
    )
    projection_update = lax.all_gather(update, "ctx", axis=0, tiled=True)
    return (attention, query_grad, key_grad, projection_update)


def solution(mesh):
    in_specs = (
        P(("dp", "ctx"), None),
        P(("dp", "ctx"), None),
        P(("dp", "ctx"), None),
        P(("dp", "ctx"), None),
        P(("dp", "ctx"), None),
        P("dp", None),
        P(("dp", "ctx"), None),
        P(("dp", "ctx"), None),
    )
    out_specs = (
        P(("dp", "ctx"), None),
        P(("dp", "ctx"), None),
        P(("dp", "ctx"), None),
        P("dp", None),
    )
    return jax.shard_map(body, mesh=mesh, in_specs=in_specs, out_specs=out_specs, check_vma=False)
```

profile of v0, /device:TPU:6, one launch (start us, length us, event | category | flops | bytes accessed | tf_op | source)
XLA Modules:
  0.0 1733.9 jit_solution(14945301684018893414)
XLA Ops:
  10.2 11.4 all-to-all-start
  24.6 29.4 %all-to-all-done = bf16[128,16,256]{0,2,1:T(8,128)(2,1)} async-done(((bf16[128,16,256]{0,2,1:T(8,128)(2,1)}), bf16[128,16,256]{0,2,1:T(8,128)(2,1)}, u32[]{:S(2)}, u32[]{:S(2)}) %all-to-all-start) | async-done | bytes 1048608 | tf_op jit(solution)/shard_map/all_to_all | solution.py:152
  67.3 27.6 %all-to-all-done.2 = bf16[128,16,256]{0,2,1:T(8,128)(2,1)} async-done(((bf16[128,16,256]{0,2,1:T(8,128)(2,1)}), bf16[128,16,256]{0,2,1:T(8,128)(2,1)}, u32[]{:S(2)}, u32[]{:S(2)}) %all-to-all-start.2) | async-done | bytes 1048608 | tf_op jit(solution)/shard_map/all_to_all | solution.py:153
  106.3 57.2 %all-gather.3.cloned.1.call-done = bf16[2048,512]{1,0:T(8,128)(2,1)} async-done(((bf16[128,512]{1,0:T(8,128)(2,1)}), bf16[2048,512]{1,0:T(8,128)(2,1)}) %all-gather.3.cloned.1.call-update) | async-done | bytes 2097168 | tf_op jit(solution)/shard_map/all_gather | solution.py:156
  164.6 20.1 %while.133 = (s32[]{:T(128)}, f32[2,2048]{1,0:T(2,128)S(1)}, s32[2048]{0:T(1024)S(1)}, bf16[2048,2,128]{2,0,1:T(8,128)(2,1)}, bf16[2048,128]{1,0:T(8,128)(2,1)S(...) while((s32[]{:T(128)}, f32[2,2048]{1,0:T(2,128)S(1)}, ...), condition=%wide.region_5.6_spmd, body=%wide.region_0.5_spmd.sunk | while | flops 139202560 | bytes 5992962 | solution.py:56
  185.8 34.7 %while.135 = (s32[]{:T(128)}, bf16[2048,2,128]{0,2,1:T(8,128)(2,1)}, s32[2048]{0:T(1024)S(1)}, bf16[2048,2,128]{2,0,1:T(8,128)(2,1)}, f32[2,2048]{1,0:T(2,128)S(...) while((s32[]{:T(128)}, bf16[2048,2,128]{0,2,1:T(8,128)(2,1)}, ...), condition=%wide.region_9.10_spmd, body=%wide.region_6.9_spmd.sunk | while | flops 272106496 | bytes 3966478 | solution.py:79
  200.1 7.3 while.139
  210.0 9.7 while.139
  225.6 77.7 %while.137 = (s32[]{:T(128)}, f32[2048,2,128]{2,0,1:T(8,128)}, bf16[2048,128]{1,0:T(8,128)(2,1)}, bf16[2048,128]{1,0:T(8,128)(2,1)}, bf16[2048,128]{1,0:T(8,128)...) while((s32[]{:T(128)}, f32[2048,2,128]{2,0,1:T(8,128)}, ...), condition=%wide.region_14.15_spmd, body=%wide.region_11.14_spmd.sunk | while | flops 676660224 | bytes 19837592 | solution.py:131
  226.6 28.2 %while.140 = (s32[]{:T(128)}, f32[2048,2,128]{2,0,1:T(8,128)}, f32[512,128]{1,0:T(8,128)S(1)}, f32[512,128]{1,0:T(8,128)S(1)}, s32[]{:T(128)}, /*index=5*/s32[20...) while((s32[]{:T(128)}, f32[2048,2,128]{2,0,1:T(8,128)}, ...), condition=%wide.region_13.13_spmd, body=%wide.region_12.12_spmd.sunk | while | flops 676463616 | bytes 17998092 | solution.py:115
  256.6 21.1 %while.140 = (s32[]{:T(128)}, f32[2048,2,128]{2,0,1:T(8,128)}, f32[512,128]{1,0:T(8,128)S(1)}, f32[512,128]{1,0:T(8,128)S(1)}, s32[]{:T(128)}, /*index=5*/s32[20...) while((s32[]{:T(128)}, f32[2048,2,128]{2,0,1:T(8,128)}, ...), condition=%wide.region_13.13_spmd, body=%wide.region_12.12_spmd.sunk | while | flops 676463616 | bytes 17998092 | solution.py:115
  279.6 14.1 while.140
  295.5 7.1 while.140
  303.3 21.1 %all_to_all.102 = bf16[16,128,128]{2,1,0:T(8,128)(2,1)S(1)} all-to-all(bf16[16,128,128]{2,1,0:T(8,128)(2,1)} %bitcast.165), channel_id=1, replica_groups=mesh['dp'=16,'ctx'=16] {'ctx'}, dimensions={0} | all-to-all | bytes 1048576 | tf_op jit(solution)/shard_map/all_to_all | solution.py:169
  324.6 8.1 convolution_bitcast_fusion.2
  332.6 17.4 %copy.123 = f32[8192,512]{1,0:T(8,128)} copy(f32[8192,512]{0,1:T(8,128)} %convolution_bitcast_fusion.2) | data formatting | bytes 33554432
  350.1 6.6 all-to-all-start.4
  361.5 13.2 all-to-all-done.4
  374.8 6.5 all-to-all-start.1
  389.0 21.4 %all-to-all-done.1 = bf16[16,128,256]{2,1,0:T(8,128)(2,1)} async-done(((bf16[16,128,256]{2,1,0:T(8,128)(2,1)}), bf16[16,128,256]{2,1,0:T(8,128)(2,1)}, u32[]{:S(2)}, u32[]{:S(2)}) %all-to-all-start.1) | async-done | bytes 1048608 | tf_op jit(solution)/shard_map/all_to_all | solution.py:166
  410.4 7.8 all-to-all-start.3
  423.8 15.2 all-to-all-done.3
  441.2 1230.0 %reduce-scatter.4.cloned.1.call-done = f32[32,512]{1,0:T(8,128)} async-done(((f32[8192,512]{1,0:T(8,128)}), f32[32,512]{1,0:T(8,128)}) %reduce-scatter.4.cloned.1.call-update) | async-done | bytes 65552 | tf_op jit(solution)/shard_map/reduce_scatter | solution.py:175
  1672.1 54.5 %all_gather.11 = bf16[512,512]{1,0:T(8,128)(2,1)S(1)} all-gather(bf16[32,512]{1,0:T(8,128)(2,1)S(1)} %fusion.55), channel_id=1, replica_groups=mesh['dp'=16,'ctx'=16] {'ctx'}, dimensions={0}, use_global_device_ids=true | all-gather | bytes 557056 | tf_op jit(solution)/shard_map/all_gather | solution.py:188
  (349 shorter events, 213.5 us)
Async XLA Ops:
  7.2 317.4 %copy-start = (bf16[128,8192]{1,0:T(8,128)(2,1)S(1)}, bf16[128,8192]{1,0:T(8,128)(2,1)}, u32[]{:S(2)}) copy-start(bf16[128,8192]{1,0:T(8,128)(2,1)} %param.20) | copy-start | bytes 6291460
  7.2 95.2 %all-gather.5.cloned.1.call-start = ((), (), s32[]{:S(2)}) async-start(), calls=%async_computation.8 | async-start | bytes 2228224 | tf_op jit(solution)/shard_map/all_gather | solution.py:157
  10.2 43.8 %all-to-all-start = ((bf16[128,16,256]{0,2,1:T(8,128)(2,1)}), bf16[128,16,256]{0,2,1:T(8,128)(2,1)}, u32[]{:S(2)}, u32[]{:S(2)}) async-start(bf16[128,16,256]{0,2,1:T(8,128)(2,1)} %bitcast.159), calls=%async_computation | async-start | bytes 2097152 | tf_op jit(solution)/shard_map/all_to_all | solution.py:152
  21.6 141.9 %all-gather.3.cloned.1.call-start = ((), (), s32[]{:S(2)}) async-start(), calls=%async_computation.7 | async-start | bytes 2228224 | tf_op jit(solution)/shard_map/all_gather | solution.py:156
  54.0 40.9 %all-to-all-start.2 = ((bf16[128,16,256]{0,2,1:T(8,128)(2,1)}), bf16[128,16,256]{0,2,1:T(8,128)(2,1)}, u32[]{:S(2)}, u32[]{:S(2)}) async-start(bf16[128,16,256]{0,2,1:T(8,128)(2,1)} %bitcast.158), calls=%async_computation.2 | async-start | bytes 2097152 | tf_op jit(solution)/shard_map/all_to_all | solution.py:153
  59.6 1611.6 %reduce-scatter.4.cloned.1.call-start = ((), (), s32[]{:S(2)}) async-start(), calls=%async_computation.9 | async-start | bytes 16842752 | tf_op jit(solution)/shard_map/reduce_scatter | solution.py:175
  102.4 62.3 %copy-start.2 = (s32[1,2048]{1,0:T(1,128)S(1)}, s32[1,2048]{1,0:T(1,128)}, u32[]{:S(2)}) copy-start(s32[1,2048]{1,0:T(1,128)} %param.25) | copy-start | bytes 24580
  227.0 2.0 copy-start.1
  234.1 2.0 copy-start.1
  241.1 2.0 copy-start.1
  248.1 2.0 copy-start.1
  257.0 2.0 copy-start.1
  264.0 2.0 copy-start.1
  271.1 2.0 copy-start.1
  279.9 2.0 copy-start.1
  287.0 2.0 copy-start.1
  295.9 2.0 copy-start.1
  350.1 24.7 %all-to-all-start.4 = ((bf16[16,128,128]{2,1,0:T(8,128)(2,1)}), bf16[16,128,128]{2,1,0:T(8,128)(2,1)S(1)}, u32[]{:S(2)}, u32[]{:S(2)}) async-start(bf16[16,128,128]{2,1,0:T(8,128)(2,1)} %bitcast.23), calls=%async_computation.4 | async-start | bytes 1048576 | tf_op jit(solution)/shard_map/all_to_all | solution.py:168
  374.8 35.6 %all-to-all-start.1 = ((bf16[16,128,256]{2,1,0:T(8,128)(2,1)}), bf16[16,128,256]{2,1,0:T(8,128)(2,1)}, u32[]{:S(2)}, u32[]{:S(2)}) async-start(bf16[16,128,256]{2,1,0:T(8,128)(2,1)} %copy.122), calls=%async_computation.1 | async-start | bytes 2097152 | tf_op jit(solution)/shard_map/all_to_all | solution.py:166
  410.4 28.5 %all-to-all-start.3 = ((bf16[16,128,256]{1,2,0:T(8,128)(2,1)}), bf16[16,128,256]{1,2,0:T(8,128)(2,1)}, u32[]{:S(2)}, u32[]{:S(2)}) async-start(bf16[16,128,256]{1,2,0:T(8,128)(2,1)} %copy.110), calls=%async_computation.3 | async-start | bytes 2097152 | tf_op jit(solution)/shard_map/all_to_all | solution.py:167
  421.4 1249.8 %copy-start.3 = (f32[32,512]{1,0:T(8,128)S(1)}, f32[32,512]{1,0:T(8,128)}, u32[]{:S(2)}) copy-start(f32[32,512]{1,0:T(8,128)} %param.27) | copy-start | bytes 196612
  421.4 1249.8 %copy-start.4 = (f32[32,512]{1,0:T(8,128)S(1)}, f32[32,512]{1,0:T(8,128)}, u32[]{:S(2)}) copy-start(f32[32,512]{1,0:T(8,128)} %param.26) | copy-start | bytes 196612
Sparse Core Ops, SparseCore 0:
  10.4 90.0 all-gather.4
  103.0 60.4 all-gather.2
  350.2 1320.9 reduce-scatter.3
where the time goes:
time: 1740 us; the launch traced here: 1730 us
  waiting for transfers between devices  1400 us (80%)
  matrix products  100 us (6%)
  local copies, waits for them, and re-layouts  82.8 us (5%)
  blocking collectives  75.5 us (4%)
  starting transfers between devices  38 us (2%)
  other arithmetic  25.9 us (1%)
    reduce_scatter x1, waiting for transfers between devices, body(): lax.psum_scatter(lax.dot_general(layer_input, value_grad, (((0,), (0,)),...  1230 us
    all_gather x1, waiting for transfers between devices, body(): lax.all_gather(layer_keys, 'ctx', axis=0, tiled=True)  57.2 us
    all_gather x1, blocking collectives, body(): projection_update = lax.all_gather(update, 'ctx', axis=0, tiled=True)  54.5 us
  transfers between devices with their start and end apart: 8, of which 7 were waited for; matrix products, arithmetic and copies ran while one was open for 3% of the time, Pallas kernels for 0%

commit v1 on v0

v1 whole, which is shorter than its diff:
```python
import functools

import jax
import jax.numpy as jnp
from jax import lax
from jax.experimental import pallas as pl
from jax.experimental.pallas import tpu as pltpu
from jax.sharding import PartitionSpec as P

HQ = 32
HK = 4
HD = 128
GROUP = HQ // HK
BLK = 128
NB = 5
SPAN = NB * BLK
WIDE = 2 * HD
SCALE = HD**-0.5
LOG2E = 1.4426950408889634

first_fix = 1.0 - 0.9**8
second_fix = 1.0 - 0.999**8

NT = (((1,), (1,)), ((), ()))


def build_bias(me, n_ctx, seg_ref, bias_ref):
    rows = lax.broadcasted_iota(jnp.int32, (BLK, BLK), 0)
    cols = lax.broadcasted_iota(jnp.int32, (BLK, BLK), 1)
    own = seg_ref[0:1, pl.ds(pl.multiple_of(me * BLK, BLK), BLK)]
    for slot in range(NB):
        back = NB - 1 - slot
        block = lax.rem(me - back + n_ctx, n_ctx)
        theirs = seg_ref[0:1, pl.ds(pl.multiple_of(block * BLK, BLK), BLK)]
        column = jnp.sum(
            jnp.where(rows == cols, jnp.broadcast_to(theirs, (BLK, BLK)), 0).astype(jnp.float32),
            axis=1,
            keepdims=True,
        )
        allowed = column == own.astype(jnp.float32)
        if back == 0:
            allowed = allowed & (rows <= cols)
        else:
            allowed = allowed & (jnp.full((BLK, BLK), me, jnp.int32) >= back)
        bias = jnp.where(allowed, 0.0, -1e30)
        bias_ref[slot * BLK : (slot + 1) * BLK, 0:HD] = bias
        bias_ref[slot * BLK : (slot + 1) * BLK, HD:WIDE] = bias


def lanes(index):
    return pl.ds(pl.multiple_of(index * HD, HD), HD)


def pair_rows(ref, head):
    return jnp.concatenate([ref[:, lanes(head)], ref[:, lanes(head + 1)]], axis=0)


def group_rows(ref, g):
    return jnp.concatenate([ref[:, lanes(g * GROUP + i)] for i in range(GROUP)], axis=0)


def probs_of_group(g, q_ref, k_ref, bias_ref, prob_ref):
    k_head = k_ref[:, lanes(g)]
    for pair in range(GROUP // 2):
        head = g * GROUP + 2 * pair
        raw = lax.dot_general(
            k_head, pair_rows(q_ref, head), NT, preferred_element_type=jnp.float32
        )
        masked = raw + bias_ref[...]
        top = jnp.max(masked, axis=0, keepdims=True)
        grown = jnp.exp2((masked - top) * (SCALE * LOG2E))
        total = jnp.sum(grown, axis=0, keepdims=True)
        probs = grown * (1.0 / total)
        prob_ref[g, :, pair * WIDE : (pair + 1) * WIDE] = probs.astype(jnp.bfloat16)


def value_part(g, prob_ref, go_ref):
    return jnp.dot(prob_ref[g], group_rows(go_ref, g), preferred_element_type=jnp.float32)


def grads_of_group(g, q_ref, k_ref, v_ref, go_ref, prob_ref, ds_ref, out_ref, dq_ref):
    k_head = k_ref[:, lanes(g)]
    v_head = v_ref[:, lanes(g)]
    k_turned = k_head.T
    v_turned = v_head.T
    for pair in range(GROUP // 2):
        head = g * GROUP + 2 * pair
        cut = slice(pair * WIDE, (pair + 1) * WIDE)
        low = prob_ref[g, :, cut]
        dprobs = lax.dot_general(
            v_head, pair_rows(go_ref, head), NT, preferred_element_type=jnp.float32
        )
        probs = low.astype(jnp.float32)
        delta = jnp.sum(probs * dprobs, axis=0, keepdims=True)
        ds = (probs * (dprobs - delta)).astype(jnp.bfloat16)
        ds_ref[:, cut] = ds
        out_t = jnp.dot(v_turned, low, preferred_element_type=jnp.float32)
        dq_t = jnp.dot(k_turned, ds, preferred_element_type=jnp.float32) * SCALE
        for i in range(2):
            part = slice(i * HD, (i + 1) * HD)
            out_ref[:, lanes(head + i)] = out_t[:, part].T.astype(jnp.bfloat16)
            dq_ref[:, lanes(head + i)] = dq_t[:, part].T.astype(jnp.bfloat16)
    return (
        jnp.dot(ds_ref[...], group_rows(q_ref, g), preferred_element_type=jnp.float32) * SCALE
    )


def attention_kernel(
    n_ctx, q_ref, k_ref, v_ref, go_ref, seg_ref, out_ref, dq_ref, dk_ref, dv_ref,
    bias_ref, prob_ref, ds_ref,
):
    me = lax.axis_index("ctx")
    build_bias(me, n_ctx, seg_ref, bias_ref)

    @pl.loop(0, HK)
    def _(g):
        probs_of_group(g, q_ref, k_ref, bias_ref, prob_ref)
        dv_ref[:, lanes(g)] = value_part(g, prob_ref, go_ref).astype(jnp.bfloat16)

    @pl.loop(0, HK)
    def _(g):
        dk = grads_of_group(
            g, q_ref, k_ref, v_ref, go_ref, prob_ref, ds_ref, out_ref, dq_ref
        )
        dk_ref[:, lanes(g)] = dk.astype(jnp.bfloat16)


def attend(q, k, v, go, seg, n_ctx):
    bf = jnp.bfloat16
    whole = pl.BlockSpec(memory_space=pltpu.VMEM)
    return pl.pallas_call(
        functools.partial(attention_kernel, n_ctx),
        out_shape=(
            jax.ShapeDtypeStruct(q.shape, bf),
            jax.ShapeDtypeStruct(q.shape, bf),
            jax.ShapeDtypeStruct((SPAN, HK * HD), bf),
            jax.ShapeDtypeStruct((SPAN, HK * HD), bf),
        ),
        in_specs=[whole] * 5,
        out_specs=(whole,) * 4,
        scratch_shapes=[
            pltpu.VMEM((SPAN, WIDE), jnp.float32),
            pltpu.VMEM((HK, SPAN, GROUP * HD), bf),
            pltpu.VMEM((SPAN, GROUP * HD), bf),
        ],
        compiler_params=pltpu.CompilerParams(vmem_limit_bytes=48 * 1024 * 1024),
        cost_estimate=pl.CostEstimate(
            flops=2 * 6 * HQ * BLK * SPAN * HD, bytes_accessed=8 << 20, transcendentals=HQ * BLK * SPAN
        ),
    )(q, k, v, go, seg)


def body(
    layer_input, queries, layer_keys, layer_values, output_grad, segment_ids, first_moment, second_moment
):
    n_ctx = lax.axis_size("ctx")
    tok = queries.shape[0]

    def shifted(x, by):
        return lax.ppermute(x, "ctx", [(i, (i + by) % n_ctx) for i in range(n_ctx)])

    both = jnp.concatenate([layer_keys, layer_values], axis=1)
    spans = [shifted(both, by) for by in range(NB - 1, 0, -1)] + [both]
    spans = jnp.concatenate(spans, axis=0)
    k_span, v_span = spans[:, : HK * HD], spans[:, HK * HD :]
    inputs = lax.all_to_all(layer_input, "dp", split_axis=1, concat_axis=0, tiled=True)
    attention, query_grad, dk_part, dv_part = attend(
        queries, k_span, v_span, output_grad, segment_ids, n_ctx
    )
    parts = jnp.concatenate([dk_part, dv_part], axis=1)
    total = parts[(NB - 1) * tok :].astype(jnp.float32)
    for by in range(1, NB):
        slot = NB - 1 - by
        total = total + shifted(parts[slot * tok : (slot + 1) * tok], -by).astype(jnp.float32)
    total = total.astype(jnp.bfloat16)
    key_grad, value_grad = total[:, : HK * HD], total[:, HK * HD :]
    values_all = lax.all_gather(value_grad, "dp", axis=0, tiled=True)
    partial = lax.dot_general(
        inputs, values_all, (((0,), (0,)), ((), ())), preferred_element_type=jnp.float32
    )
    gradient = lax.psum_scatter(partial, "ctx", scatter_dimension=0, tiled=True)
    new_first = 0.9 * first_moment + 0.1 * gradient
    new_second = 0.999 * second_moment + 0.001 * gradient * gradient
    update = (new_first / first_fix / (jnp.sqrt(new_second / second_fix) + 1e-08)).astype(
        jnp.bfloat16
    )
    projection_update = lax.all_gather(update, "ctx", axis=0, tiled=True)
    return (attention, query_grad, key_grad, projection_update)


def solution(mesh):
    rows = P(("dp", "ctx"), None)
    in_specs = (rows, rows, rows, rows, rows, P("dp", None), rows, rows)
    out_specs = (rows, rows, rows, P("dp", None))
    return jax.shard_map(body, mesh=mesh, in_specs=in_specs, out_specs=out_specs, check_vma=False)
```

time: 1740 us -> 278 us (0.16)
  the two profiles are of different devices: /device:TPU:6 before, /device:TPU:16 now
where the time goes in v1:
time: 278 us; the launch traced here: 277 us
  waiting for transfers between devices  154 us (55%)
  blocking collectives  45.7 us (16%)
  starting transfers between devices  29 us (10%)
  Pallas kernels  16.1 us (6%)
  between operations  14.2 us (5%)
  local copies, waits for them, and re-layouts  12.6 us (5%)
  matrix products  3.49 us (1%)
    reduce_scatter x1, waiting for transfers between devices, body(): gradient = lax.psum_scatter(partial, 'ctx', scatter_dimension=0, tiled=True)  84.7 us
    all_gather x1, blocking collectives, body(): projection_update = lax.all_gather(update, 'ctx', axis=0, tiled=True)  45.7 us
    ppermute x8, waiting for transfers between devices, shifted(): return lax.ppermute(x, 'ctx', [(i, (i + by) % n_ctx) for i in range(n_ctx)])  29.5 us
    ppermute x8, starting transfers between devices, shifted(): return lax.ppermute(x, 'ctx', [(i, (i + by) % n_ctx) for i in range(n_ctx)])  23 us
    all_to_all x1, waiting for transfers between devices, body(): lax.all_to_all(layer_input, 'dp', split_axis=1, concat_axis=0, tiled=True)  21.5 us
    all_gather x1, waiting for transfers between devices, body(): values_all = lax.all_gather(value_grad, 'dp', axis=0, tiled=True)  18.1 us
    pallas_call x1, Pallas kernels, attend(): pl.pallas_call(functools.partial(attention_kernel, n_ctx), out_shape=(jax...  16.1 us
    unnamed x26, local copies, waits for them, and re-layouts  7.15 us
  transfers between devices with their start and end apart: 11, of which 8 were waited for; matrix products, arithmetic and copies ran while one was open for 3% of the time, Pallas kernels for 0%

profile of v1, /device:TPU:16, one launch (start us, length us, event | category | flops | bytes accessed | tf_op | source)
XLA Modules:
  0.0 277.2 jit_solution(8907325011329649815)
XLA Ops:
  7.2 1.0 constant_dynamic-update-slice_fusion.1
  9.1 1.6 collective-permute-start
  10.7 6.3 %collective-permute-start.1 = (bf16[128,1024]{1,0:T(8,128)(2,1)S(1)}, bf16[128,1024]{1,0:T(8,128)(2,1)S(1)}, u32[]{:S(2)}, u32[]{:S(2)}) collective-permute-start(bf16[128,1024]{1,0:T(8,128)(2,1)S(1)} %constant_dynamic-update-slice_fusion), channel_id=1, source_target_pairs={{0,3},{1,4},{2,5},{3,6},{4,7},{5,8},{6,9},{7,10},{8,11},{9,12},{10... | collective-permute-start | bytes 786440 | tf_op jit(solution)/shard_map/ppermute | solution.py:160
  17.0 1.5 collective-permute-start.2
  18.5 3.3 %collective-permute-start.3 = (bf16[128,1024]{1,0:T(8,128)(2,1)S(1)}, bf16[128,1024]{1,0:T(8,128)(2,1)S(1)}, u32[]{:S(2)}, u32[]{:S(2)}) collective-permute-start(bf16[128,1024]{1,0:T(8,128)(2,1)S(1)} %constant_dynamic-update-slice_fusion), channel_id=1, source_target_pairs={{0,1},{1,2},{2,3},{3,4},{4,5},{5,6},{6,7},{7,8},{8,9},{9,10},{10,1... | collective-permute-start | bytes 786440 | tf_op jit(solution)/shard_map/ppermute | solution.py:160
  21.8 17.4 %collective-permute-done.1 = bf16[128,1024]{1,0:T(8,128)(2,1)S(1)} collective-permute-done((bf16[128,1024]{1,0:T(8,128)(2,1)S(1)}, bf16[128,1024]{1,0:T(8,128)(2,1)S(1)}, u32[]{:S(2)}, u32[]{:S(2)}) %collective-permute-start.1) | collective-permute-done | bytes 262176 | tf_op jit(solution)/shard_map/ppermute | solution.py:160
  40.1 2.0 collective-permute-done.3
  42.3 1.1 copy-done
  43.7 16.1 %shard_map.111 = (bf16[128,4096]{1,0:T(8,128)(2,1)}, bf16[128,4096]{1,0:T(8,128)(2,1)}, bf16[640,512]{1,0:T(8,128)(2,1)S(1)}, bf16[640,512]{1,0:T(8,128)(2,1)S(1)}) custom-call(bf16[128,4096]{1,0:T(8,128)(2,1)S(1)} %copy-done, bf16[640,512]{1,0:T(8,128)(2,1)S(1)} %get-tuple-element.29.k_ref, bf16[640,512]{1,0:T(8,128)(2,1)S(1)} %get-tuple-element.28.v_ref, ...), custom_call_target="tpu_custom_call" | custom-call | flops 4026531840 | bytes 8388608 | tf_op jit(solution)/shard_map/pallas_call | solution.py:131
  60.1 1.0 fusion.6
  61.1 5.7 %collective-permute-start.4 = (bf16[128,1024]{1,0:T(8,128)(2,1)}, bf16[128,1024]{1,0:T(8,128)(2,1)}, u32[]{:S(2)}, u32[]{:S(2)}) collective-permute-start(bf16[128,1024]{1,0:T(8,128)(2,1)} %get-tuple-element.24), channel_id=1, source_target_pairs={{0,15},{1,0},{2,1},{3,2},{4,3},{5,4},{6,5},{7,6},{8,7},{9,8},{10,9... | collective-permute-start | bytes 786440 | tf_op jit(solution)/shard_map/ppermute | solution.py:160
  66.7 4.7 %collective-permute-start.5 = (bf16[128,1024]{1,0:T(8,128)(2,1)}, bf16[128,1024]{1,0:T(8,128)(2,1)}, u32[]{:S(2)}, u32[]{:S(2)}) collective-permute-start(bf16[128,1024]{1,0:T(8,128)(2,1)} %get-tuple-element.27), channel_id=1, source_target_pairs={{0,14},{1,15},{2,0},{3,1},{4,2},{5,3},{6,4},{7,5},{8,6},{9,7},{10,... | collective-permute-start | bytes 786440 | tf_op jit(solution)/shard_map/ppermute | solution.py:160
  71.5 2.4 copy.28
  73.9 5.9 %all-to-all-start = ((bf16[128,16,512]{0,2,1:T(8,128)(2,1)}), bf16[128,16,512]{0,2,1:T(8,128)(2,1)S(1)}, u32[]{:S(2)}, u32[]{:S(2)}) async-start(bf16[128,16,512]{0,2,1:T(8,128)(2,1)} %bitcast.9), calls=%async_computation | async-start | bytes 4194304 | tf_op jit(solution)/shard_map/all_to_all | solution.py:166
  79.8 5.2 %collective-permute-done.4 = bf16[128,1024]{1,0:T(8,128)(2,1)} collective-permute-done((bf16[128,1024]{1,0:T(8,128)(2,1)}, bf16[128,1024]{1,0:T(8,128)(2,1)}, u32[]{:S(2)}, u32[]{:S(2)}) %collective-permute-start.4) | collective-permute-done | bytes 262176 | tf_op jit(solution)/shard_map/ppermute | solution.py:160
  85.0 4.0 %collective-permute-done.6 = bf16[128,1024]{1,0:T(8,128)(2,1)} collective-permute-done((bf16[128,1024]{1,0:T(8,128)(2,1)}, bf16[128,1024]{1,0:T(8,128)(2,1)}, u32[]{:S(2)}, u32[]{:S(2)}) %collective-permute-start.6) | collective-permute-done | bytes 262176 | tf_op jit(solution)/shard_map/ppermute | solution.py:160
  89.1 1.4 add_convert_fusion
  91.2 21.5 %all-to-all-done = bf16[128,16,512]{0,2,1:T(8,128)(2,1)S(1)} async-done(((bf16[128,16,512]{0,2,1:T(8,128)(2,1)}), bf16[128,16,512]{0,2,1:T(8,128)(2,1)S(1)}, u32[]{:S(2)}, u32[]{:S(2)}) %all-to-all-start) | async-done | bytes 2097184 | tf_op jit(solution)/shard_map/all_to_all | solution.py:166
  112.8 2.6 copy.29
  115.4 18.1 %all-gather.2.cloned.1.call-done = bf16[2048,512]{1,0:T(8,128)(2,1)} async-done(((bf16[128,512]{1,0:T(8,128)(2,1)}), bf16[2048,512]{1,0:T(8,128)(2,1)}) %all-gather.2.cloned.1.call-update) | async-done | bytes 2097168 | tf_op jit(solution)/shard_map/all_gather | solution.py:177
  133.5 3.5 %convolution_bitcast_fusion = f32[512,512]{0,1:T(8,128)S(1)} fusion(bf16[2048,512]{1,0:T(8,128)(2,1)} %all-gather.2.cloned.1.call-done, bf16[2048,512]{1,0:T(8,128)(2,1)} %bitcast.10), kind=kOutput, calls=%fused_computation | convolution fusion | flops 1073741824 | bytes 5242880 | tf_op jit(solution)/shard_map/dot_general | solution.py:178
  137.0 1.3 copy.33
  138.4 84.7 %reduce-scatter.4.cloned.1.call-done = f32[32,512]{1,0:T(8,128)} async-done(((f32[512,512]{1,0:T(8,128)}), f32[32,512]{1,0:T(8,128)}) %reduce-scatter.4.cloned.1.call-update) | async-done | bytes 65552 | tf_op jit(solution)/shard_map/reduce_scatter | solution.py:181
  223.9 45.7 %all_gather.7 = bf16[512,512]{1,0:T(8,128)(2,1)S(1)} all-gather(bf16[32,512]{1,0:T(8,128)(2,1)S(1)} %fusion.5), channel_id=1, replica_groups=mesh['dp'=16,'ctx'=16] {'ctx'}, dimensions={0}, use_global_device_ids=true | all-gather | bytes 557056 | tf_op jit(solution)/shard_map/all_gather | solution.py:187
  (38 shorter events, 5.1 us)
Async XLA Ops:
  7.2 35.0 %copy-start.4 = (bf16[128,512]{1,0:T(8,128)(2,1)S(1)}, bf16[128,512]{1,0:T(8,128)(2,1)}, u32[]{:S(2)}) copy-start(bf16[128,512]{1,0:T(8,128)(2,1)} %param.10) | copy-start | bytes 393220
  8.2 34.0 %copy-start.5 = (bf16[128,512]{1,0:T(8,128)(2,1)S(1)}, bf16[128,512]{1,0:T(8,128)(2,1)}, u32[]{:S(2)}) copy-start(bf16[128,512]{1,0:T(8,128)(2,1)} %param.11) | copy-start | bytes 393220
  9.1 12.6 %collective-permute-start = (bf16[128,1024]{1,0:T(8,128)(2,1)S(1)}, bf16[128,1024]{1,0:T(8,128)(2,1)S(1)}, u32[]{:S(2)}, u32[]{:S(2)}) collective-permute-start(bf16[128,1024]{1,0:T(8,128)(2,1)S(1)} %constant_dynamic-update-slice_fusion), channel_id=1, source_target_pairs={{0,4},{1,5},{2,6},{3,7},{4,8},{5,9},{6,10},{7,11},{8,12},{9,13},{1... | collective-permute-start | bytes 786440 | tf_op jit(solution)/shard_map/ppermute | solution.py:160
  10.7 28.5 %collective-permute-start.1 = (bf16[128,1024]{1,0:T(8,128)(2,1)S(1)}, bf16[128,1024]{1,0:T(8,128)(2,1)S(1)}, u32[]{:S(2)}, u32[]{:S(2)}) collective-permute-start(bf16[128,1024]{1,0:T(8,128)(2,1)S(1)} %constant_dynamic-update-slice_fusion), channel_id=1, source_target_pairs={{0,3},{1,4},{2,5},{3,6},{4,7},{5,8},{6,9},{7,10},{8,11},{9,12},{10... | collective-permute-start | bytes 786440 | tf_op jit(solution)/shard_map/ppermute | solution.py:160
  17.0 23.1 %collective-permute-start.2 = (bf16[128,1024]{1,0:T(8,128)(2,1)S(1)}, bf16[128,1024]{1,0:T(8,128)(2,1)S(1)}, u32[]{:S(2)}, u32[]{:S(2)}) collective-permute-start(bf16[128,1024]{1,0:T(8,128)(2,1)S(1)} %constant_dynamic-update-slice_fusion), channel_id=1, source_target_pairs={{0,2},{1,3},{2,4},{3,5},{4,6},{5,7},{6,8},{7,9},{8,10},{9,11},{10,... | collective-permute-start | bytes 786440 | tf_op jit(solution)/shard_map/ppermute | solution.py:160
  18.5 23.6 %collective-permute-start.3 = (bf16[128,1024]{1,0:T(8,128)(2,1)S(1)}, bf16[128,1024]{1,0:T(8,128)(2,1)S(1)}, u32[]{:S(2)}, u32[]{:S(2)}) collective-permute-start(bf16[128,1024]{1,0:T(8,128)(2,1)S(1)} %constant_dynamic-update-slice_fusion), channel_id=1, source_target_pairs={{0,1},{1,2},{2,3},{3,4},{4,5},{5,6},{6,7},{7,8},{8,9},{9,10},{10,1... | collective-permute-start | bytes 786440 | tf_op jit(solution)/shard_map/ppermute | solution.py:160
  42.2 1.2 copy-start
  42.2 1.5 copy-start.1
  42.2 1.5 copy-start.2
  60.0 11.4 %copy-start.3 = (bf16[128,8192]{1,0:T(8,128)(2,1)S(1)}, bf16[128,8192]{1,0:T(8,128)(2,1)}, u32[]{:S(2)}) copy-start(bf16[128,8192]{1,0:T(8,128)(2,1)} %param.8) | copy-start | bytes 6291460
  61.1 24.0 %collective-permute-start.4 = (bf16[128,1024]{1,0:T(8,128)(2,1)}, bf16[128,1024]{1,0:T(8,128)(2,1)}, u32[]{:S(2)}, u32[]{:S(2)}) collective-permute-start(bf16[128,1024]{1,0:T(8,128)(2,1)} %get-tuple-element.24), channel_id=1, source_target_pairs={{0,15},{1,0},{2,1},{3,2},{4,3},{5,4},{6,5},{7,6},{8,7},{9,8},{10,9... | collective-permute-start | bytes 786440 | tf_op jit(solution)/shard_map/ppermute | solution.py:160
  66.7 18.3 %collective-permute-start.7 = (bf16[128,1024]{1,0:T(8,128)(2,1)}, bf16[128,1024]{1,0:T(8,128)(2,1)}, u32[]{:S(2)}, u32[]{:S(2)}) collective-permute-start(bf16[128,1024]{1,0:T(8,128)(2,1)} %get-tuple-element.25), channel_id=1, source_target_pairs={{0,12},{1,13},{2,14},{3,15},{4,0},{5,1},{6,2},{7,3},{8,4},{9,5},{1... | collective-permute-start | bytes 786440 | tf_op jit(solution)/shard_map/ppermute | solution.py:160
  66.7 22.3 %collective-permute-start.6 = (bf16[128,1024]{1,0:T(8,128)(2,1)}, bf16[128,1024]{1,0:T(8,128)(2,1)}, u32[]{:S(2)}, u32[]{:S(2)}) collective-permute-start(bf16[128,1024]{1,0:T(8,128)(2,1)} %get-tuple-element.26), channel_id=1, source_target_pairs={{0,13},{1,14},{2,15},{3,0},{4,1},{5,2},{6,3},{7,4},{8,5},{9,6},{10... | collective-permute-start | bytes 786440 | tf_op jit(solution)/shard_map/ppermute | solution.py:160
  66.7 22.3 %collective-permute-start.5 = (bf16[128,1024]{1,0:T(8,128)(2,1)}, bf16[128,1024]{1,0:T(8,128)(2,1)}, u32[]{:S(2)}, u32[]{:S(2)}) collective-permute-start(bf16[128,1024]{1,0:T(8,128)(2,1)} %get-tuple-element.27), channel_id=1, source_target_pairs={{0,14},{1,15},{2,0},{3,1},{4,2},{5,3},{6,4},{7,5},{8,6},{9,7},{10,... | collective-permute-start | bytes 786440 | tf_op jit(solution)/shard_map/ppermute | solution.py:160
  73.9 38.9 %all-to-all-start = ((bf16[128,16,512]{0,2,1:T(8,128)(2,1)}), bf16[128,16,512]{0,2,1:T(8,128)(2,1)S(1)}, u32[]{:S(2)}, u32[]{:S(2)}) async-start(bf16[128,16,512]{0,2,1:T(8,128)(2,1)} %bitcast.9), calls=%async_computation | async-start | bytes 4194304 | tf_op jit(solution)/shard_map/all_to_all | solution.py:166
  79.8 53.7 %all-gather.2.cloned.1.call-start = ((), (), s32[]{:S(2)}) async-start(), calls=%async_computation.2 | async-start | bytes 2228224 | tf_op jit(solution)/shard_map/all_gather | solution.py:177
  91.2 131.8 %reduce-scatter.4.cloned.1.call-start = ((), (), s32[]{:S(2)}) async-start(), calls=%async_computation.3 | async-start | bytes 1114112 | tf_op jit(solution)/shard_map/reduce_scatter | solution.py:181
  137.0 86.1 %copy-start.6 = (f32[32,512]{1,0:T(8,128)S(1)}, f32[32,512]{1,0:T(8,128)}, u32[]{:S(2)}) copy-start(f32[32,512]{1,0:T(8,128)} %param.15) | copy-start | bytes 196612
  137.0 86.0 %copy-start.7 = (f32[32,512]{1,0:T(8,128)S(1)}, f32[32,512]{1,0:T(8,128)}, u32[]{:S(2)}) copy-start(f32[32,512]{1,0:T(8,128)} %param.14) | copy-start | bytes 196612
Sparse Core Ops, SparseCore 0:
  91.3 42.1 all-gather.1
  138.5 84.4 reduce-scatter.3

commit v2 on v1

--- a/solution.py
+++ b/solution.py
@@ -1,5 +1,3 @@
-import functools
-
 import jax
 import jax.numpy as jnp
 from jax import lax
@@ -105,87 +103,374 @@
     )
 
 
-def attention_kernel(
-    n_ctx, q_ref, k_ref, v_ref, go_ref, seg_ref, out_ref, dq_ref, dk_ref, dv_ref,
-    bias_ref, prob_ref, ds_ref,
+MESH = pl.DeviceIdType.MESH
+N_CTX = 16
+N_X = 4
+N_ZH = 4
+N_Y = 4
+ROWS = 32
+WIDTH = HK * HD
+
+
+def remote(src, dst, send_sem, recv_sem, dp, ctx):
+    return pltpu.make_async_remote_copy(
+        src_ref=src,
+        dst_ref=dst,
+        send_sem=send_sem,
+        recv_sem=recv_sem,
+        device_id=(dp, ctx),
+        device_id_type=MESH,
+    )
+
+
+def step_kernel(
+    x_ref, q_ref, k_ref, v_ref, go_ref, seg_ref, m_ref, s_ref,
+    out_ref, dq_ref, dk_ref, up_ref,
+    bias_ref, prob_ref, ds_ref, out_v, dq_v, k_span, v_span, dv_part, dk_part, dv_got, dk_got,
+    xs_ref, xt_ref, vg_ref, sx_ref, rx_ref, acc_ref, sz_ref, rz_ref, up_v,
+    halo_s, halo_r, x_s, x_r, x_l, dv_s, dv_r, dk_s, dk_r, vg_s, vg_r,
+    rx_s, rx_r, rz_s, rz_r, ag_s, ag_r, out_l,
 ):
+    bf = jnp.bfloat16
+    dp = lax.axis_index("dp")
     me = lax.axis_index("ctx")
-    build_bias(me, n_ctx, seg_ref, bias_ref)
+    y, zl, core = dp // 4, (dp // 2) % 2, dp % 2
+    x, zh = me // N_ZH, me % N_ZH
+
+    def ctx_at(by):
+        return (me + by + N_CTX) % N_CTX
+
+    def share_at(dy, dc):
+        return ((y + dy) % N_Y) * 4 + zl * 2 + (core + dc) % 2
+
+    def x_at(dx):
+        return ((x + dx) % N_X) * N_ZH + zh
+
+    def z_at(dh):
+        return x * N_ZH + (zh + dh) % N_ZH
+
+    def zl_at(dl):
+        return y * 4 + ((zl + dl) % 2) * 2 + core
+
+    partners = [(dp, ctx_at(by)) for by in (1, 2, 3, 4, -1, -2, -3, -4, 8)]
+    partners += [(share_at(e // 2, e % 2), me) for e in range(1, 8)]
+    partners += [(zl_at(1), z_at(dh)) for dh in range(N_ZH)]
+    barrier = pltpu.get_barrier_semaphore()
+    for partner in partners:
+        pl.semaphore_signal(barrier, inc=1, device_id=partner, device_id_type=MESH)
+    pl.semaphore_wait(barrier, len(partners))
+
+    def halo(which, by):
+        src, span = ((k_ref, k_span), (v_ref, v_span))[which]
+        slot = NB - 1 - by
+        return remote(
+            src,
+            span.at[pl.ds(slot * BLK, BLK), :],
+            halo_s.at[which, by - 1],
+            halo_r.at[which, by - 1],
+            dp,
+            ctx_at(by),
+        )
+
+    def x_share(e, j):
+        dy, dc = e // 2, e % 2
+        first = (((y + dy) % N_Y) * 4 + j * 2 + (core + dc) % 2) * 512
+        src = x_ref.at[:, pl.ds(pl.multiple_of(first, 512), 512)]
+        dst = xs_ref.at[e, :, pl.ds(j * 512, 512)]
+        if e == 0:
+            return pltpu.make_async_copy(src, dst, x_l.at[j])
+        return remote(src, dst, x_s.at[e, j], x_r.at[e, j], share_at(dy, dc), me)
+
+    for which in range(2):
+        for by in range(1, NB):
+            halo(which, by).start()
+    for e in (1, 2, 3, 6, 7, 4, 5, 0):
+        for j in range(2):
+            x_share(e, j).start()
+
+    k_span[(NB - 1) * BLK :, :] = k_ref[...]
+    v_span[(NB - 1) * BLK :, :] = v_ref[...]
+    build_bias(me, N_CTX, seg_ref, bias_ref)
+
+    def back(part, got, send, recv, g, by):
+        slot = NB - 1 - by
+        return remote(
+            part.at[pl.ds(slot * BLK, BLK), lanes(g)],
+            got.at[by - 1, :, lanes(g)],
+            send.at[g, by - 1],
+            recv.at[g, by - 1],
+            dp,
+            ctx_at(-by),
+        )
+
+    for by in range(1, NB):
+        halo(0, by).wait_recv()
 
     @pl.loop(0, HK)
     def _(g):
-        probs_of_group(g, q_ref, k_ref, bias_ref, prob_ref)
-        dv_ref[:, lanes(g)] = value_part(g, prob_ref, go_ref).astype(jnp.bfloat16)
+        probs_of_group(g, q_ref, k_span, bias_ref, prob_ref)
+        dv_part[:, lanes(g)] = value_part(g, prob_ref, go_ref).astype(bf)
+        for by in range(1, NB):
+            back(dv_part, dv_got, dv_s, dv_r, g, by).start()
+
+    for by in range(1, NB):
+        halo(1, by).wait_recv()
+
+    def grads(first, last):
+        @pl.loop(first, last)
+        def _(g):
+            dk = grads_of_group(
+                g, q_ref, k_span, v_span, go_ref, prob_ref, ds_ref, out_v, dq_v
+            )
+            dk_part[:, lanes(g)] = dk.astype(bf)
+            for by in range(1, NB):
+                back(dk_part, dk_got, dk_s, dk_r, g, by).start()
+
+    grads(0, 2)
+
+    def gathered(part, got, send, recv):
+        @pl.loop(0, HK)
+        def _(g):
+            for by in range(1, NB):
+                back(part, got, send, recv, g, by).wait_recv()
+        total = part[(NB - 1) * BLK :, :].astype(jnp.float32)
+        for by in range(1, NB):
+            total = total + got[by - 1].astype(jnp.float32)
+        return total.astype(bf)
+
+    vg_ref[0] = gathered(dv_part, dv_got, dv_s, dv_r)
+
+    def vg_send(dy):
+        return remote(
+            vg_ref.at[0], vg_ref.at[2 * dy], vg_s.at[2 * dy], vg_r.at[2 * dy], share_at(dy, 0), me
+        )
+
+    def vg_pass(dy):
+        return remote(
+            vg_ref.at[2 * dy],
+            vg_ref.at[2 * dy + 1],
+            vg_s.at[2 * dy + 1],
+            vg_r.at[2 * dy + 1],
+            share_at(0, 1),
+            me,
+        )
+
+    for dy in range(1, N_Y):
+        vg_send(dy).start()
+    vg_pass(0).start()
+
+    for e in range(8):
+        for j in range(2):
+            if e == 0:
+                x_share(e, j).wait()
+            else:
+                x_share(e, j).wait_recv()
+
+    @pl.loop(0, 8)
+    def _(e):
+        xt_ref[:, lanes(e)] = xs_ref[e].T
+
+    grads(2, HK)
+    copies = (
+        pltpu.make_async_copy(out_v, out_ref, out_l.at[0]),
+        pltpu.make_async_copy(dq_v, dq_ref, out_l.at[1]),
+    )
+    for copy in copies:
+        copy.start()
+
+    for dy in range(1, N_Y):
+        vg_send(dy).wait_recv()
+        vg_pass(dy).start()
+    for dy in range(N_Y):
+        vg_pass(dy).wait_recv()
+
+    def x_piece(d, j):
+        return remote(
+            sx_ref.at[d, pl.ds(j * 128, 128), :],
+            rx_ref.at[d, pl.ds(j * 128, 128), :],
+            rx_s.at[d, j],
+            rx_r.at[d, j],
+            dp,
+            x_at(d),
+        )
+
+    def partial_for(d):
+        first = ((x + d) % N_X) * 128
+        left = jnp.concatenate(
+            [xt_ref[pl.ds(pl.multiple_of(j * 512 + first, 128), 128), :] for j in range(2)], axis=0
+        )
+        return jnp.dot(
+            left, vg_ref[...].reshape(8 * BLK, WIDTH), preferred_element_type=jnp.float32
+        )
+
+    for d in (2, 1, 3):
+        sx_ref[d] = partial_for(d).astype(bf)
+        for j in range(2):
+            x_piece(d, j).start()
+    acc_ref[...] = partial_for(0)
+
+    for d in (2, 1, 3):
+        for j in range(2):
+            x_piece(d, j).wait_recv()
+    acc_ref[...] = (
+        acc_ref[...]
+        + rx_ref[1].astype(jnp.float32)
+        + rx_ref[2].astype(jnp.float32)
+        + rx_ref[3].astype(jnp.float32)
+    )
+    sz_ref[...] = acc_ref[...].astype(bf)
+
+    def z_rows(dl, dh):
+        first = ((zl + dl) % 2) * 128 + ((zh + dh) % N_ZH) * ROWS
+        return pl.ds(pl.multiple_of(first, ROWS), ROWS)
+
+    def z_piece(e):
+        dl, dh = e % 2, e // 2
+        return remote(
+            sz_ref.at[z_rows(dl, dh), :], rz_ref.at[e], rz_s.at[e], rz_r.at[e], zl_at(dl), z_at(dh)
+        )
+
+    for e in (4, 5, 3, 2, 6, 7, 1):
+        z_piece(e).start()
+
+    dk_ref[...] = gathered(dk_part, dk_got, dk_s, dk_r)
+
+    for e in range(1, 8):
+        z_piece(e).wait_recv()
+    gradient = acc_ref[z_rows(0, 0), :]
+    for e in range(1, 8):
+        gradient = gradient + rz_ref[e].astype(jnp.float32)
+    new_first = 0.9 * m_ref[...] + 0.1 * gradient
+    new_second = 0.999 * s_ref[...] + 0.001 * gradient * gradient
+    update = new_first / first_fix / (jnp.sqrt(new_second / second_fix) + 1e-08)
+
+    def up_rows(dh):
+        return up_v.at[pl.ds(pl.multiple_of(z_at(dh) * ROWS, ROWS), ROWS), :]
+
+    up_v[pl.ds(pl.multiple_of(me * ROWS, ROWS), ROWS), :] = update.astype(bf)
+
+    def along_z(dh):
+        return remote(up_rows(0), up_rows(0), ag_s.at[0, dh], ag_r.at[0, dh], dp, z_at(dh))
+
+    def along_x(dx, dh):
+        return remote(up_rows(-dh), up_rows(-dh), ag_s.at[dx, dh], ag_r.at[dx, dh], dp, x_at(dx))
+
+    for dh in (2, 1, 3):
+        along_z(dh).start()
+    for dx in (2, 1, 3):
+        along_x(dx, 0).start()
+    for dh in (1, 3, 2):
+        along_z(dh).wait_recv()
+        for dx in (2, 1, 3):
+            along_x(dx, dh).start()
+    for dx in range(1, N_X):
+        for dh in range(N_ZH):
+            along_x(dx, dh).wait_recv()
+    last = pltpu.make_async_copy(up_v, up_ref, out_l.at[2])
+    last.start()
+
+    for which in range(2):
+        for by in range(1, NB):
+            halo(which, by).wait_send()
+    for e in range(1, 8):
+        for j in range(2):
+            x_share(e, j).wait_send()
 
     @pl.loop(0, HK)
     def _(g):
-        dk = grads_of_group(
-            g, q_ref, k_ref, v_ref, go_ref, prob_ref, ds_ref, out_ref, dq_ref
-        )
-        dk_ref[:, lanes(g)] = dk.astype(jnp.bfloat16)
-
-
-def attend(q, k, v, go, seg, n_ctx):
-    bf = jnp.bfloat16
-    whole = pl.BlockSpec(memory_space=pltpu.VMEM)
-    return pl.pallas_call(
-        functools.partial(attention_kernel, n_ctx),
-        out_shape=(
-            jax.ShapeDtypeStruct(q.shape, bf),
-            jax.ShapeDtypeStruct(q.shape, bf),
-            jax.ShapeDtypeStruct((SPAN, HK * HD), bf),
-            jax.ShapeDtypeStruct((SPAN, HK * HD), bf),
-        ),
-        in_specs=[whole] * 5,
-        out_specs=(whole,) * 4,
-        scratch_shapes=[
-            pltpu.VMEM((SPAN, WIDE), jnp.float32),
-            pltpu.VMEM((HK, SPAN, GROUP * HD), bf),
-            pltpu.VMEM((SPAN, GROUP * HD), bf),
-        ],
-        compiler_params=pltpu.CompilerParams(vmem_limit_bytes=48 * 1024 * 1024),
-        cost_estimate=pl.CostEstimate(
-            flops=2 * 6 * HQ * BLK * SPAN * HD, bytes_accessed=8 << 20, transcendentals=HQ * BLK * SPAN
-        ),
-    )(q, k, v, go, seg)
+        for by in range(1, NB):
+            back(dv_part, dv_got, dv_s, dv_r, g, by).wait_send()
+            back(dk_part, dk_got, dk_s, dk_r, g, by).wait_send()
+
+    for dy in range(1, N_Y):
+        vg_send(dy).wait_send()
+    for dy in range(N_Y):
+        vg_pass(dy).wait_send()
+    for d in range(1, N_X):
+        for j in range(2):
+            x_piece(d, j).wait_send()
+    for e in range(1, 8):
+        z_piece(e).wait_send()
+    for dh in range(1, N_ZH):
+        along_z(dh).wait_send()
+    for dx in range(1, N_X):
+        for dh in range(N_ZH):
+            along_x(dx, dh).wait_send()
+    for copy in copies:
+        copy.wait()
+    last.wait()
 
 
 def body(
     layer_input, queries, layer_keys, layer_values, output_grad, segment_ids, first_moment, second_moment
 ):
-    n_ctx = lax.axis_size("ctx")
-    tok = queries.shape[0]
-
-    def shifted(x, by):
-        return lax.ppermute(x, "ctx", [(i, (i + by) % n_ctx) for i in range(n_ctx)])
-
-    both = jnp.concatenate([layer_keys, layer_values], axis=1)
-    spans = [shifted(both, by) for by in range(NB - 1, 0, -1)] + [both]
-    spans = jnp.concatenate(spans, axis=0)
-    k_span, v_span = spans[:, : HK * HD], spans[:, HK * HD :]
-    inputs = lax.all_to_all(layer_input, "dp", split_axis=1, concat_axis=0, tiled=True)
-    attention, query_grad, dk_part, dv_part = attend(
-        queries, k_span, v_span, output_grad, segment_ids, n_ctx
+    bf = jnp.bfloat16
+    f32 = jnp.float32
+    whole = pl.BlockSpec(memory_space=pltpu.VMEM)
+    far = pl.BlockSpec(memory_space=pl.ANY)
+    dma = pltpu.SemaphoreType.DMA
+    return pl.pallas_call(
+        step_kernel,
+        out_shape=(
+            jax.ShapeDtypeStruct(queries.shape, bf),
+            jax.ShapeDtypeStruct(queries.shape, bf),
+            jax.ShapeDtypeStruct(layer_keys.shape, bf),
+            jax.ShapeDtypeStruct((N_CTX * ROWS, WIDTH), bf),
+        ),
+        in_specs=[far] + [whole] * 7,
+        out_specs=(far, far, whole, far),
+        scratch_shapes=[
+            pltpu.VMEM((SPAN, WIDE), f32),
+            pltpu.VMEM((HK, SPAN, GROUP * HD), bf),
+            pltpu.VMEM((SPAN, GROUP * HD), bf),
+            pltpu.VMEM((BLK, HQ * HD), bf),
+            pltpu.VMEM((BLK, HQ * HD), bf),
+            pltpu.VMEM((SPAN, WIDTH), bf),
+            pltpu.VMEM((SPAN, WIDTH), bf),
+            pltpu.VMEM((SPAN, WIDTH), bf),
+            pltpu.VMEM((SPAN, WIDTH), bf),
+            pltpu.VMEM((NB - 1, BLK, WIDTH), bf),
+            pltpu.VMEM((NB - 1, BLK, WIDTH), bf),
+            pltpu.VMEM((8, BLK, 1024), bf),
+            pltpu.VMEM((1024, 8 * BLK), bf),
+            pltpu.VMEM((8, BLK, WIDTH), bf),
+            pltpu.VMEM((N_X, 256, WIDTH), bf),
+            pltpu.VMEM((N_X, 256, WIDTH), bf),
+            pltpu.VMEM((256, WIDTH), f32),
+            pltpu.VMEM((256, WIDTH), bf),
+            pltpu.VMEM((8, ROWS, WIDTH), bf),
+            pltpu.VMEM((N_CTX * ROWS, WIDTH), bf),
+            dma((2, NB - 1)),
+            dma((2, NB - 1)),
+            dma((8, 2)),
+            dma((8, 2)),
+            dma((2,)),
+            dma((HK, NB - 1)),
+            dma((HK, NB - 1)),
+            dma((HK, NB - 1)),
+            dma((HK, NB - 1)),
+            dma((8,)),
+            dma((8,)),
+            dma((N_X, 2)),
+            dma((N_X, 2)),
+            dma((8,)),
+            dma((8,)),
+            dma((N_X, N_ZH)),
+            dma((N_X, N_ZH)),
+            dma((3,)),
+        ],
+        compiler_params=pltpu.CompilerParams(
+            collective_id=0, has_side_effects=True, vmem_limit_bytes=48 * 1024 * 1024
+        ),
+        cost_estimate=pl.CostEstimate(
+            flops=2 * 6 * HQ * BLK * SPAN * HD,
+            bytes_accessed=8 << 20,
+            transcendentals=HQ * BLK * SPAN,
+        ),
+    )(
+        layer_input, queries, layer_keys, layer_values, output_grad, segment_ids, first_moment,
+        second_moment,
     )
-    parts = jnp.concatenate([dk_part, dv_part], axis=1)
-    total = parts[(NB - 1) * tok :].astype(jnp.float32)
-    for by in range(1, NB):
-        slot = NB - 1 - by
-        total = total + shifted(parts[slot * tok : (slot + 1) * tok], -by).astype(jnp.float32)
-    total = total.astype(jnp.bfloat16)
-    key_grad, value_grad = total[:, : HK * HD], total[:, HK * HD :]
-    values_all = lax.all_gather(value_grad, "dp", axis=0, tiled=True)
-    partial = lax.dot_general(
-        inputs, values_all, (((0,), (0,)), ((), ())), preferred_element_type=jnp.float32
-    )
-    gradient = lax.psum_scatter(partial, "ctx", scatter_dimension=0, tiled=True)
-    new_first = 0.9 * first_moment + 0.1 * gradient
-    new_second = 0.999 * second_moment + 0.001 * gradient * gradient
-    update = (new_first / first_fix / (jnp.sqrt(new_second / second_fix) + 1e-08)).astype(
-        jnp.bfloat16
-    )
-    projection_update = lax.all_gather(update, "ctx", axis=0, tiled=True)
-    return (attention, query_grad, key_grad, projection_update)
 
 
 def solution(mesh):

time: 278 us -> 106 us (0.38)
  the two profiles are of different devices: /device:TPU:16 before, /device:TPU:6 now
where the time goes in v2:
time: 106 us; the launch traced here: 104 us
  Pallas kernels  93.5 us (88%)
  local copies, waits for them, and re-layouts  10 us (9%)
    pallas_call x1, Pallas kernels, body(): pl.pallas_call(step_kernel, out_shape=(jax.ShapeDtypeStruct(queries.shape...  93.5 us
    unnamed x18, local copies, waits for them, and re-layouts  10 us

profile of v2, /device:TPU:6, one launch (start us, length us, event | category | flops | bytes accessed | tf_op | source)
XLA Modules:
  0.0 104.2 jit_solution(16504742461323000751)
XLA Ops:
  0.6 0.0 copy-start
  0.6 1.2 %copy-done = bf16[128,4096]{1,0:T(8,128)(2,1)S(1)} copy-done((bf16[128,4096]{1,0:T(8,128)(2,1)S(1)}, bf16[128,4096]{1,0:T(8,128)(2,1)}, u32[]{:S(2)}) %copy-start) | copy-done | bytes 1048600
  1.9 0.0 copy-start.1
  1.9 1.2 %copy-done.1 = bf16[128,4096]{1,0:T(8,128)(2,1)S(1)} copy-done((bf16[128,4096]{1,0:T(8,128)(2,1)S(1)}, bf16[128,4096]{1,0:T(8,128)(2,1)}, u32[]{:S(2)}) %copy-start.1) | copy-done | bytes 1048600
  3.1 0.0 copy-start.2
  3.1 0.9 copy-done.2
  4.0 0.0 copy-start.3
  4.0 0.9 copy-done.3
  4.9 0.0 copy-start.4
  4.9 0.8 copy-done.4
  5.7 0.0 copy-start.5
  5.7 0.8 copy-done.5
  6.6 0.0 copy-start.6
  6.6 0.7 copy-done.6
  7.3 93.5 %shard_map.111 = (bf16[128,4096]{1,0:T(8,128)(2,1)S(1)}, bf16[128,4096]{1,0:T(8,128)(2,1)S(1)}, bf16[128,512]{1,0:T(8,128)(2,1)S(1)}, bf16[512,512]{1,0:T(8,128)(2,1)S(1)}) custom-call(bf16[128,8192]{1,0:T(8,128)(2,1)} %x_ref.1, bf16[128,4096]{1,0:T(8,128)(2,1)S(1)} %copy-done, bf16[128,512]{1,0:T(8,128)(2,1)S(1)} %copy-done.2, ...), custom_call_target="tpu_custom_call" | custom-call | flops 4026531840 | bytes 8388608 | tf_op jit(solution)/shard_map/pallas_call | solution.py:412
  100.8 1.0 copy.16
  101.7 1.0 copy.17
  102.7 0.7 copy.18
  103.4 0.8 copy.19
Async XLA Ops:
  0.6 1.2 %copy-start = (bf16[128,4096]{1,0:T(8,128)(2,1)S(1)}, bf16[128,4096]{1,0:T(8,128)(2,1)}, u32[]{:S(2)}) copy-start(bf16[128,4096]{1,0:T(8,128)(2,1)} %q_ref.1) | copy-start | bytes 3145732
  1.9 1.2 %copy-start.1 = (bf16[128,4096]{1,0:T(8,128)(2,1)S(1)}, bf16[128,4096]{1,0:T(8,128)(2,1)}, u32[]{:S(2)}) copy-start(bf16[128,4096]{1,0:T(8,128)(2,1)} %go_ref.1) | copy-start | bytes 3145732
  3.1 0.9 copy-start.2
  4.0 0.9 copy-start.3
  4.9 0.8 copy-start.4
  5.7 0.8 copy-start.5
  6.6 0.7 copy-start.6

commit v3 on v2

v3 whole, which is shorter than its diff:
```python
import jax
import jax.numpy as jnp
from jax import lax
from jax.experimental import pallas as pl
from jax.experimental.pallas import tpu as pltpu
from jax.sharding import PartitionSpec as P

HQ = 32
HK = 4
HD = 128
GROUP = HQ // HK
BLK = 128
NB = 5
SPAN = NB * BLK
WIDE = 2 * HD
SCALE = HD**-0.5
LOG2E = 1.4426950408889634

first_fix = 1.0 - 0.9**8
second_fix = 1.0 - 0.999**8

NT = (((1,), (1,)), ((), ()))


def build_bias(me, n_ctx, seg_ref, bias_ref):
    rows = lax.broadcasted_iota(jnp.int32, (BLK, BLK), 0)
    cols = lax.broadcasted_iota(jnp.int32, (BLK, BLK), 1)
    own = seg_ref[0:1, pl.ds(pl.multiple_of(me * BLK, BLK), BLK)]
    for slot in range(NB):
        back = NB - 1 - slot
        block = lax.rem(me - back + n_ctx, n_ctx)
        theirs = seg_ref[0:1, pl.ds(pl.multiple_of(block * BLK, BLK), BLK)]
        column = jnp.sum(
            jnp.where(rows == cols, jnp.broadcast_to(theirs, (BLK, BLK)), 0).astype(jnp.float32),
            axis=1,
            keepdims=True,
        )
        allowed = column == own.astype(jnp.float32)
        if back == 0:
            allowed = allowed & (rows <= cols)
        else:
            allowed = allowed & (jnp.full((BLK, BLK), me, jnp.int32) >= back)
        bias = jnp.where(allowed, 0.0, -1e30)
        bias_ref[slot * BLK : (slot + 1) * BLK, 0:HD] = bias
        bias_ref[slot * BLK : (slot + 1) * BLK, HD:WIDE] = bias


def lanes(index):
    return pl.ds(pl.multiple_of(index * HD, HD), HD)


def pair_rows(ref, head):
    return jnp.concatenate([ref[:, lanes(head)], ref[:, lanes(head + 1)]], axis=0)


def group_rows(ref, g):
    return jnp.concatenate([ref[:, lanes(g * GROUP + i)] for i in range(GROUP)], axis=0)


def probs_of_group(g, q_ref, k_ref, bias_ref, prob_ref):
    k_head = k_ref[:, lanes(g)]
    for pair in range(GROUP // 2):
        head = g * GROUP + 2 * pair
        raw = lax.dot_general(
            k_head, pair_rows(q_ref, head), NT, preferred_element_type=jnp.float32
        )
        masked = raw + bias_ref[...]
        top = jnp.max(masked, axis=0, keepdims=True)
        grown = jnp.exp2((masked - top) * (SCALE * LOG2E))
        total = jnp.sum(grown, axis=0, keepdims=True)
        probs = grown * (1.0 / total)
        prob_ref[g, :, pair * WIDE : (pair + 1) * WIDE] = probs.astype(jnp.bfloat16)


def value_part(g, prob_ref, go_ref):
    return jnp.dot(prob_ref[g], group_rows(go_ref, g), preferred_element_type=jnp.float32)


def grads_of_group(g, q_ref, k_ref, v_ref, go_ref, prob_ref, ds_ref, out_ref, dq_ref):
    k_head = k_ref[:, lanes(g)]
    v_head = v_ref[:, lanes(g)]
    k_turned = k_head.T
    v_turned = v_head.T
    for pair in range(GROUP // 2):
        head = g * GROUP + 2 * pair
        cut = slice(pair * WIDE, (pair + 1) * WIDE)
        low = prob_ref[g, :, cut]
        dprobs = lax.dot_general(
            v_head, pair_rows(go_ref, head), NT, preferred_element_type=jnp.float32
        )
        probs = low.astype(jnp.float32)
        delta = jnp.sum(probs * dprobs, axis=0, keepdims=True)
        ds = (probs * (dprobs - delta)).astype(jnp.bfloat16)
        ds_ref[:, cut] = ds
        out_t = jnp.dot(v_turned, low, preferred_element_type=jnp.float32)
        dq_t = jnp.dot(k_turned, ds, preferred_element_type=jnp.float32) * SCALE
        for i in range(2):
            part = slice(i * HD, (i + 1) * HD)
            out_ref[:, lanes(head + i)] = out_t[:, part].T.astype(jnp.bfloat16)
            dq_ref[:, lanes(head + i)] = dq_t[:, part].T.astype(jnp.bfloat16)
    return (
        jnp.dot(ds_ref[...], group_rows(q_ref, g), preferred_element_type=jnp.float32) * SCALE
    )


MESH = pl.DeviceIdType.MESH
N_CTX = 16
N_X = 4
N_ZH = 4
N_Y = 4
ROWS = 32
WIDTH = HK * HD
HALF = WIDTH // 2


def remote(src, dst, send_sem, recv_sem, dp, ctx):
    return pltpu.make_async_remote_copy(
        src_ref=src,
        dst_ref=dst,
        send_sem=send_sem,
        recv_sem=recv_sem,
        device_id=(dp, ctx),
        device_id_type=MESH,
    )


def step_kernel(
    x_ref, q_hbm, k_hbm, v_hbm, go_hbm, seg_hbm, m_hbm, s_hbm,
    out_ref, dq_ref, dk_ref, up_ref,
    q_ref, go_ref, seg_ref, m_ref, s_ref,
    bias_ref, prob_ref, ds_ref, out_v, dq_v, k_span, v_span, dv_part, dk_part, dv_got, dk_got,
    xs_ref, xt_ref, vg_ref, sx_ref, rx_ref, acc_ref, sz_ref, rz_ref, up_v, dk_v,
    load_l, halo_s, halo_r, x_s, x_r, x_l, dv_s, dv_r, dk_s, dk_r, vg_s, vg_r,
    rx_s, rx_r, rz_s, rz_r, ag_s, ag_r, out_l,
):
    bf = jnp.bfloat16
    f32 = jnp.float32
    dp = lax.axis_index("dp")
    me = lax.axis_index("ctx")
    y, zl, core = dp // 4, (dp // 2) % 2, dp % 2
    x, zh = me // N_ZH, me % N_ZH
    own_rows = pl.ds((NB - 1) * BLK, BLK)

    loads = [
        pltpu.make_async_copy(src, dst, load_l.at[i])
        for i, (src, dst) in enumerate(
            (
                (seg_hbm, seg_ref),
                (k_hbm, k_span.at[own_rows, :]),
                (q_hbm, q_ref),
                (go_hbm, go_ref),
                (v_hbm, v_span.at[own_rows, :]),
                (m_hbm, m_ref),
                (s_hbm, s_ref),
            )
        )
    ]
    for load in loads:
        load.start()

    def ctx_at(by):
        return (me + by + N_CTX) % N_CTX

    def share_at(dy, dc):
        return ((y + dy) % N_Y) * 4 + zl * 2 + (core + dc) % 2

    def x_at(dx):
        return ((x + dx) % N_X) * N_ZH + zh

    def z_at(dh):
        return x * N_ZH + (zh + dh + N_ZH) % N_ZH

    def zl_at(dl):
        return y * 4 + ((zl + dl) % 2) * 2 + core

    partners = [(dp, ctx_at(by)) for by in (1, 2, 3, 4, -1, -2, -3, -4, 8)]
    partners += [(share_at(e // 2, e % 2), me) for e in range(1, 8)]
    partners += [(zl_at(1), z_at(dh)) for dh in range(N_ZH)]
    barrier = pltpu.get_barrier_semaphore()
    for partner in partners:
        pl.semaphore_signal(barrier, inc=1, device_id=partner, device_id_type=MESH)
    pl.semaphore_wait(barrier, len(partners))

    def halo(which, g, by):
        src, span = ((k_hbm, k_span), (v_hbm, v_span))[which]
        slot = NB - 1 - by
        return remote(
            src.at[:, lanes(g)],
            span.at[pl.ds(slot * BLK, BLK), lanes(g)],
            halo_s.at[which, g, by - 1],
            halo_r.at[which, g, by - 1],
            dp,
            ctx_at(by),
        )

    def x_share(e, j):
        dy, dc = e // 2, e % 2
        first = (((y + dy) % N_Y) * 4 + j * 2 + (core + dc) % 2) * 512
        src = x_ref.at[:, pl.ds(pl.multiple_of(first, 512), 512)]
        dst = xs_ref.at[e, :, pl.ds(j * 512, 512)]
        if e == 0:
            return pltpu.make_async_copy(src, dst, x_l.at[j])
        return remote(src, dst, x_s.at[e, j], x_r.at[e, j], share_at(dy, dc), me)

    def back(part, got, send, recv, g, by):
        slot = NB - 1 - by
        return remote(
            part.at[pl.ds(slot * BLK, BLK), lanes(g)],
            got.at[by - 1, :, lanes(g)],
            send.at[g, by - 1],
            recv.at[g, by - 1],
            dp,
            ctx_at(-by),
        )

    def dv_back(g, by):
        return back(dv_part, dv_got, dv_s, dv_r, g, by)

    def dk_back(g, by):
        return back(dk_part, dk_got, dk_s, dk_r, g, by)

    def send_spans(which, first, last):
        @pl.loop(first, last)
        def _(g):
            for by in range(1, NB):
                halo(which, g, by).start()

    def probs(first, last):
        @pl.loop(first, last)
        def _(g):
            for by in range(1, NB):
                halo(0, g, by).wait_recv()
            probs_of_group(g, q_ref, k_span, bias_ref, prob_ref)
            dv_part[:, lanes(g)] = value_part(g, prob_ref, go_ref).astype(bf)
            for by in range(1, NB):
                dv_back(g, by).start()

    def grads(first, last):
        @pl.loop(first, last)
        def _(g):
            for by in range(1, NB):
                halo(1, g, by).wait_recv()
            dk = grads_of_group(
                g, q_ref, k_span, v_span, go_ref, prob_ref, ds_ref, out_v, dq_v
            )
            dk_part[:, lanes(g)] = dk.astype(bf)
            for by in range(1, NB):
                dk_back(g, by).start()

    def columns(h):
        return pl.ds(h * HALF, HALF)

    def sum_values(h):
        for g in (2 * h, 2 * h + 1):
            for by in range(1, NB):
                dv_back(g, by).wait_recv()
        total = dv_part[own_rows, columns(h)].astype(f32)
        for by in range(1, NB):
            total = total + dv_got[by - 1, :, columns(h)].astype(f32)
        vg_ref[h, 0] = total.astype(bf)

    def vg_send(h, dy):
        e = 2 * dy
        return remote(
            vg_ref.at[h, 0], vg_ref.at[h, e], vg_s.at[h, e], vg_r.at[h, e], share_at(dy, 0), me
        )

    def vg_pass(h, dy):
        e = 2 * dy
        return remote(
            vg_ref.at[h, e],
            vg_ref.at[h, e + 1],
            vg_s.at[h, e + 1],
            vg_r.at[h, e + 1],
            share_at(0, 1),
            me,
        )

    def gather_values(h):
        for dy in (2, 1, 3):
            vg_send(h, dy).start()
        vg_pass(h, 0).start()

    def pass_values(h):
        for dy in (1, 3, 2):
            vg_send(h, dy).wait_recv()
            vg_pass(h, dy).start()

    def turn_inputs():
        for e in range(8):
            for j in range(2):
                if e == 0:
                    x_share(e, j).wait()
                else:
                    x_share(e, j).wait_recv()

        @pl.loop(0, 8)
        def _(e):
            xt_ref[:, lanes(e)] = xs_ref[e].T

    def x_piece(h, d):
        return remote(
            sx_ref.at[h, d], rx_ref.at[h, d], rx_s.at[h, d], rx_r.at[h, d], dp, x_at(d)
        )

    def partial_for(h, d):
        first = ((x + d) % N_X) * 128
        left = jnp.concatenate(
            [xt_ref[pl.ds(pl.multiple_of(j * 512 + first, 128), 128), :] for j in range(2)], axis=0
        )
        return jnp.dot(left, vg_ref[h].reshape(8 * BLK, HALF), preferred_element_type=f32)

    def partials(h):
        for dy in range(N_Y):
            vg_pass(h, dy).wait_recv()
        for d in (2, 1, 3):
            sx_ref[h, d] = partial_for(h, d).astype(bf)
            x_piece(h, d).start()
        acc_ref[h] = partial_for(h, 0)

    def z_rows(dl, dh):
        first = ((zl + dl) % 2) * 128 + ((zh + dh) % N_ZH) * ROWS
        return pl.ds(pl.multiple_of(first, ROWS), ROWS)

    def z_piece(h, e):
        dl, dh = e % 2, e // 2
        return remote(
            sz_ref.at[h, z_rows(dl, dh), :],
            rz_ref.at[h, e],
            rz_s.at[h, e],
            rz_r.at[h, e],
            zl_at(dl),
            z_at(dh),
        )

    def sum_x(h):
        for d in (1, 3, 2):
            x_piece(h, d).wait_recv()
        total = acc_ref[h]
        for d in range(1, N_X):
            total = total + rx_ref[h, d].astype(f32)
        acc_ref[h] = total
        sz_ref[h] = total.astype(bf)
        for e in (4, 5, 3, 2, 6, 7, 1):
            z_piece(h, e).start()

    def up_rows(h, dh):
        return up_v.at[pl.ds(pl.multiple_of(z_at(dh) * ROWS, ROWS), ROWS), columns(h)]

    def along_z(h, dh):
        return remote(
            up_rows(h, 0), up_rows(h, 0), ag_s.at[h, 0, dh], ag_r.at[h, 0, dh], dp, z_at(dh)
        )

    def along_x(h, dx, dh):
        return remote(
            up_rows(h, -dh), up_rows(h, -dh), ag_s.at[h, dx, dh], ag_r.at[h, dx, dh], dp, x_at(dx)
        )

    def adam(h):
        for e in range(1, 8):
            z_piece(h, e).wait_recv()
        gradient = acc_ref[h, z_rows(0, 0), :]
        for e in range(1, 8):
            gradient = gradient + rz_ref[h, e].astype(f32)
        new_first = 0.9 * m_ref[:, columns(h)] + 0.1 * gradient
        new_second = 0.999 * s_ref[:, columns(h)] + 0.001 * gradient * gradient
        update = new_first / first_fix / (jnp.sqrt(new_second / second_fix) + 1e-08)
        up_v[pl.ds(pl.multiple_of(me * ROWS, ROWS), ROWS), columns(h)] = update.astype(bf)
        for dh in (2, 1, 3):
            along_z(h, dh).start()
        for dx in (2, 1, 3):
            along_x(h, dx, 0).start()

    def pass_updates(h):
        for dh in (1, 3, 2):
            along_z(h, dh).wait_recv()
            for dx in (2, 1, 3):
                along_x(h, dx, dh).start()

    def sum_keys():
        @pl.loop(0, HK)
        def _(g):
            for by in range(1, NB):
                dk_back(g, by).wait_recv()

        total = dk_part[own_rows, :].astype(f32)
        for by in range(1, NB):
            total = total + dk_got[by - 1].astype(f32)
        dk_v[...] = total.astype(bf)

    outs = [
        pltpu.make_async_copy(src, dst, out_l.at[i])
        for i, (src, dst) in enumerate(
            ((out_v, out_ref), (dq_v, dq_ref), (dk_v, dk_ref), (up_v, up_ref))
        )
    ]

    send_spans(0, 0, HK)
    for e in (4, 5, 2, 3, 6, 7, 1, 0):
        for j in range(2):
            x_share(e, j).start()
    loads[0].wait()
    build_bias(me, N_CTX, seg_ref, bias_ref)
    for load in loads[1:]:
        load.wait()

    probs(0, 4)
    sum_values(0)
    gather_values(0)
    sum_values(1)
    gather_values(1)
    send_spans(1, 0, 4)
    turn_inputs()
    pass_values(0)
    partials(0)
    pass_values(1)
    partials(1)
    grads(0, 2)
    sum_x(0)
    sum_x(1)
    grads(2, 3)
    adam(0)
    adam(1)
    grads(3, 4)
    outs[0].start()
    outs[1].start()
    pass_updates(0)
    pass_updates(1)
    sum_keys()
    outs[2].start()
    for h in range(2):
        for dx in range(1, N_X):
            for dh in range(N_ZH):
                along_x(h, dx, dh).wait_recv()
    outs[3].start()

    @pl.loop(0, HK)
    def _(g):
        for by in range(1, NB):
            halo(0, g, by).wait_send()
            halo(1, g, by).wait_send()
            dv_back(g, by).wait_send()
            dk_back(g, by).wait_send()

    for e in range(1, 8):
        for j in range(2):
            x_share(e, j).wait_send()
    for h in range(2):
        for dy in range(1, N_Y):
            vg_send(h, dy).wait_send()
        for dy in range(N_Y):
            vg_pass(h, dy).wait_send()
        for d in range(1, N_X):
            x_piece(h, d).wait_send()
        for e in range(1, 8):
            z_piece(h, e).wait_send()
        for dh in range(1, N_ZH):
            along_z(h, dh).wait_send()
        for dx in range(1, N_X):
            for dh in range(N_ZH):
                along_x(h, dx, dh).wait_send()
    for out in outs:
        out.wait()


PIECES = [(i, first, 32) for i in range(2) for first in range(0, BLK, 32)]
PIECES += [(2, 0, BLK)] + [(3, first, 128) for first in range(0, 512, 128)]


def hand_over_kernel(*refs):
    ins, outs, helds = refs[0:4], refs[4:8], refs[8:12]
    in_sems, out_sems = refs[12], refs[13]
    fetches, stores = [], []
    for n, (i, first, rows) in enumerate(PIECES):
        cut = pl.ds(first, rows)
        held = helds[i].at[cut, :]
        fetches.append(pltpu.make_async_copy(ins[i].at[cut, :], held, in_sems.at[n]))
        stores.append(pltpu.make_async_copy(held, outs[i].at[cut, :], out_sems.at[n]))
    for fetch in fetches:
        fetch.start()
    for fetch, store in zip(fetches, stores):
        fetch.wait()
        store.start()
    for store in stores:
        store.wait()


def body(
    layer_input, queries, layer_keys, layer_values, output_grad, segment_ids, first_moment, second_moment
):
    bf = jnp.bfloat16
    f32 = jnp.float32
    far = pl.BlockSpec(memory_space=pl.ANY)
    vmem = pltpu.VMEM
    dma = pltpu.SemaphoreType.DMA
    results = pl.pallas_call(
        step_kernel,
        out_shape=(
            jax.ShapeDtypeStruct(queries.shape, bf),
            jax.ShapeDtypeStruct(queries.shape, bf),
            jax.ShapeDtypeStruct(layer_keys.shape, bf),
            jax.ShapeDtypeStruct((N_CTX * ROWS, WIDTH), bf),
        ),
        in_specs=[far] * 8,
        out_specs=(far,) * 4,
        scratch_shapes=[
            vmem((BLK, HQ * HD), bf),
            vmem((BLK, HQ * HD), bf),
            vmem(segment_ids.shape, jnp.int32),
            vmem((ROWS, WIDTH), f32),
            vmem((ROWS, WIDTH), f32),
            vmem((SPAN, WIDE), f32),
            vmem((HK, SPAN, GROUP * HD), bf),
            vmem((SPAN, GROUP * HD), bf),
            vmem((BLK, HQ * HD), bf),
            vmem((BLK, HQ * HD), bf),
            vmem((SPAN, WIDTH), bf),
            vmem((SPAN, WIDTH), bf),
            vmem((SPAN, WIDTH), bf),
            vmem((SPAN, WIDTH), bf),
            vmem((NB - 1, BLK, WIDTH), bf),
            vmem((NB - 1, BLK, WIDTH), bf),
            vmem((8, BLK, 1024), bf),
            vmem((1024, 8 * BLK), bf),
            vmem((2, 8, BLK, HALF), bf),
            vmem((2, N_X, 256, HALF), bf),
            vmem((2, N_X, 256, HALF), bf),
            vmem((2, 256, HALF), f32),
            vmem((2, 256, HALF), bf),
            vmem((2, 8, ROWS, HALF), bf),
            vmem((N_CTX * ROWS, WIDTH), bf),
            vmem((BLK, WIDTH), bf),
            dma((7,)),
            dma((2, HK, NB - 1)),
            dma((2, HK, NB - 1)),
            dma((8, 2)),
            dma((8, 2)),
            dma((2,)),
            dma((HK, NB - 1)),
            dma((HK, NB - 1)),
            dma((HK, NB - 1)),
            dma((HK, NB - 1)),
            dma((2, 8)),
            dma((2, 8)),
            dma((2, N_X)),
            dma((2, N_X)),
            dma((2, 8)),
            dma((2, 8)),
            dma((2, N_X, N_ZH)),
            dma((2, N_X, N_ZH)),
            dma((4,)),
        ],
        compiler_params=pltpu.CompilerParams(
            collective_id=0, has_side_effects=True, vmem_limit_bytes=60 * 1024 * 1024
        ),
        cost_estimate=pl.CostEstimate(
            flops=2 * 6 * HQ * BLK * SPAN * HD,
            bytes_accessed=8 << 20,
            transcendentals=HQ * BLK * SPAN,
        ),
    )(
        layer_input, queries, layer_keys, layer_values, output_grad, segment_ids, first_moment,
        second_moment,
    )
    return pl.pallas_call(
        hand_over_kernel,
        out_shape=tuple(jax.ShapeDtypeStruct(part.shape, part.dtype) for part in results),
        in_specs=[far] * 4,
        out_specs=(far,) * 4,
        scratch_shapes=[vmem(part.shape, part.dtype) for part in results]
        + [dma((len(PIECES),)), dma((len(PIECES),))],
        compiler_params=pltpu.CompilerParams(vmem_limit_bytes=60 * 1024 * 1024),
        cost_estimate=pl.CostEstimate(flops=0, bytes_accessed=6 << 20, transcendentals=0),
    )(*results)


def solution(mesh):
    rows = P(("dp", "ctx"), None)
    in_specs = (rows, rows, rows, rows, rows, P("dp", None), rows, rows)
    out_specs = (rows, rows, rows, P("dp", None))
    return jax.shard_map(body, mesh=mesh, in_specs=in_specs, out_specs=out_specs, check_vma=False)
```

time: 106 us -> 82.3 us (0.78); the launches traced: 104 us -> 82.2 us
  Pallas kernels: 93.5 us -> 81.5 us
  local copies, waits for them, and re-layouts: 10 us -> 0 us
    pallas_call x1, Pallas kernels: 93.5 us -> 78.8 us  [body(): pl.pallas_call(step_kernel, out_shape=(jax.ShapeDtypeStruct(queries.shape...]
    unnamed x18 -> x0, local copies, waits for them, and re-layouts: 10 us -> none
    pallas_call x0 -> x1, Pallas kernels: none -> 2.69 us  [body(): pl.pallas_call(hand_over_kernel, out_shape=tuple((jax.ShapeDtypeStruct(pa...]
where the time goes in v3:
time: 82.3 us; the launch traced here: 82.2 us
  Pallas kernels  81.5 us (99%)
    pallas_call x1, Pallas kernels, body(): pl.pallas_call(step_kernel, out_shape=(jax.ShapeDtypeStruct(queries.shape...  78.8 us
    pallas_call x1, Pallas kernels, body(): pl.pallas_call(hand_over_kernel, out_shape=tuple((jax.ShapeDtypeStruct(pa...  2.69 us

profile of v3, /device:TPU:6, one launch (start us, length us, event | category | flops | bytes accessed | tf_op | source)
XLA Modules:
  0.0 82.2 jit_solution(5444488964740791833)
XLA Ops:
  0.6 78.8 %shard_map.111 = (bf16[128,4096]{1,0:T(8,128)(2,1)}, bf16[128,4096]{1,0:T(8,128)(2,1)}, bf16[128,512]{1,0:T(8,128)(2,1)}, bf16[512,512]{1,0:T(8,128)(2,1)}) custom-call(bf16[128,8192]{1,0:T(8,128)(2,1)} %x_ref.1, bf16[128,4096]{1,0:T(8,128)(2,1)} %q_hbm.1, bf16[128,512]{1,0:T(8,128)(2,1)} %k_hbm.1, bf16[128,512]{1,0:T(8,128)(2,1)} %v_hbm.1, ...), custom_call_target="tpu_custom_call" | custom-call | flops 4026531840 | bytes 8388608 | tf_op jit(solution)/shard_map/pallas_call | solution.py:497
  79.5 2.7 %shard_map.112 = (bf16[128,4096]{1,0:T(8,128)(2,1)}, bf16[128,4096]{1,0:T(8,128)(2,1)}, bf16[128,512]{1,0:T(8,128)(2,1)}, bf16[512,512]{1,0:T(8,128)(2,1)}) custom-call(bf16[128,4096]{1,0:T(8,128)(2,1)} %get-tuple-element.8.refs_0_, bf16[128,4096]{1,0:T(8,128)(2,1)} %get-tuple-element.9.refs_1_, bf16[128,512]{1,0:T(8,128)(2,1)} %get-tuple-element.10.refs_2_, ...), custom_call_target="tpu_custom_call" | custom-call | bytes 6291456 | tf_op jit(solution)/shard_map/pallas_call | solution.py:566

commit v4 on v3

--- a/solution.py
+++ b/solution.py
@@ -126,12 +126,12 @@
 
 def step_kernel(
     x_ref, q_hbm, k_hbm, v_hbm, go_hbm, seg_hbm, m_hbm, s_hbm,
-    out_ref, dq_ref, dk_ref, up_ref,
+    out_v, dq_v, dk_v, up_v,
     q_ref, go_ref, seg_ref, m_ref, s_ref,
-    bias_ref, prob_ref, ds_ref, out_v, dq_v, k_span, v_span, dv_part, dk_part, dv_got, dk_got,
-    xs_ref, xt_ref, vg_ref, sx_ref, rx_ref, acc_ref, sz_ref, rz_ref, up_v, dk_v,
+    bias_ref, prob_ref, ds_ref, k_span, v_span, dv_part, dk_part, dv_got, dk_got,
+    xs_ref, xt_ref, vg_ref, sx_ref, rx_ref, acc_ref, sz_ref, rz_ref,
     load_l, halo_s, halo_r, x_s, x_r, x_l, dv_s, dv_r, dk_s, dk_r, vg_s, vg_r,
-    rx_s, rx_r, rz_s, rz_r, ag_s, ag_r, out_l,
+    rx_s, rx_r, rz_s, rz_r, ag_s, ag_r,
 ):
     bf = jnp.bfloat16
     f32 = jnp.float32
@@ -235,7 +235,13 @@
             for by in range(1, NB):
                 dv_back(g, by).start()
 
-    def grads(first, last):
+    def send_keys(first, last):
+        @pl.loop(first, last)
+        def _(g):
+            for by in range(1, NB):
+                dk_back(g, by).start()
+
+    def grads(first, last, send=True):
         @pl.loop(first, last)
         def _(g):
             for by in range(1, NB):
@@ -244,8 +250,9 @@
                 g, q_ref, k_span, v_span, go_ref, prob_ref, ds_ref, out_v, dq_v
             )
             dk_part[:, lanes(g)] = dk.astype(bf)
-            for by in range(1, NB):
-                dk_back(g, by).start()
+            if send:
+                for by in range(1, NB):
+                    dk_back(g, by).start()
 
     def columns(h):
         return pl.ds(h * HALF, HALF)
@@ -389,13 +396,6 @@
             total = total + dk_got[by - 1].astype(f32)
         dk_v[...] = total.astype(bf)
 
-    outs = [
-        pltpu.make_async_copy(src, dst, out_l.at[i])
-        for i, (src, dst) in enumerate(
-            ((out_v, out_ref), (dq_v, dq_ref), (dk_v, dk_ref), (up_v, up_ref))
-        )
-    ]
-
     send_spans(0, 0, HK)
     for e in (4, 5, 2, 3, 6, 7, 1, 0):
         for j in range(2):
@@ -416,24 +416,20 @@
     partials(0)
     pass_values(1)
     partials(1)
-    grads(0, 2)
+    grads(0, 3)
     sum_x(0)
     sum_x(1)
-    grads(2, 3)
+    grads(3, 4, False)
     adam(0)
     adam(1)
-    grads(3, 4)
-    outs[0].start()
-    outs[1].start()
+    send_keys(3, 4)
     pass_updates(0)
     pass_updates(1)
     sum_keys()
-    outs[2].start()
     for h in range(2):
         for dx in range(1, N_X):
             for dh in range(N_ZH):
                 along_x(h, dx, dh).wait_recv()
-    outs[3].start()
 
     @pl.loop(0, HK)
     def _(g):
@@ -460,8 +456,6 @@
         for dx in range(1, N_X):
             for dh in range(N_ZH):
                 along_x(h, dx, dh).wait_send()
-    for out in outs:
-        out.wait()
 
 
 PIECES = [(i, first, 32) for i in range(2) for first in range(0, BLK, 32)]
@@ -469,21 +463,16 @@
 
 
 def hand_over_kernel(*refs):
-    ins, outs, helds = refs[0:4], refs[4:8], refs[8:12]
-    in_sems, out_sems = refs[12], refs[13]
-    fetches, stores = [], []
-    for n, (i, first, rows) in enumerate(PIECES):
-        cut = pl.ds(first, rows)
-        held = helds[i].at[cut, :]
-        fetches.append(pltpu.make_async_copy(ins[i].at[cut, :], held, in_sems.at[n]))
-        stores.append(pltpu.make_async_copy(held, outs[i].at[cut, :], out_sems.at[n]))
-    for fetch in fetches:
-        fetch.start()
-    for fetch, store in zip(fetches, stores):
-        fetch.wait()
-        store.start()
-    for store in stores:
-        store.wait()
+    copies = [
+        pltpu.make_async_copy(
+            refs[i].at[pl.ds(first, rows), :], refs[4 + i].at[pl.ds(first, rows), :], refs[8].at[n]
+        )
+        for n, (i, first, rows) in enumerate(PIECES)
+    ]
+    for copy in copies:
+        copy.start()
+    for copy in copies:
+        copy.wait()
 
 
 def body(
@@ -492,18 +481,20 @@
     bf = jnp.bfloat16
     f32 = jnp.float32
     far = pl.BlockSpec(memory_space=pl.ANY)
+    near = pl.BlockSpec(memory_space=pltpu.VMEM)
+    hbm = pl.BlockSpec(memory_space=pltpu.HBM)
     vmem = pltpu.VMEM
     dma = pltpu.SemaphoreType.DMA
     results = pl.pallas_call(
         step_kernel,
         out_shape=(
-            jax.ShapeDtypeStruct(queries.shape, bf),
-            jax.ShapeDtypeStruct(queries.shape, bf),
-            jax.ShapeDtypeStruct(layer_keys.shape, bf),
-            jax.ShapeDtypeStruct((N_CTX * ROWS, WIDTH), bf),
+            vmem(queries.shape, bf),
+            vmem(queries.shape, bf),
+            vmem(layer_keys.shape, bf),
+            vmem((N_CTX * ROWS, WIDTH), bf),
         ),
-        in_specs=[far] * 8,
-        out_specs=(far,) * 4,
+        in_specs=[hbm] * 8,
+        out_specs=(near,) * 4,
         scratch_shapes=[
             vmem((BLK, HQ * HD), bf),
             vmem((BLK, HQ * HD), bf),
@@ -513,8 +504,6 @@
             vmem((SPAN, WIDE), f32),
             vmem((HK, SPAN, GROUP * HD), bf),
             vmem((SPAN, GROUP * HD), bf),
-            vmem((BLK, HQ * HD), bf),
-            vmem((BLK, HQ * HD), bf),
             vmem((SPAN, WIDTH), bf),
             vmem((SPAN, WIDTH), bf),
             vmem((SPAN, WIDTH), bf),
@@ -529,8 +518,6 @@
             vmem((2, 256, HALF), f32),
             vmem((2, 256, HALF), bf),
             vmem((2, 8, ROWS, HALF), bf),
-            vmem((N_CTX * ROWS, WIDTH), bf),
-            vmem((BLK, WIDTH), bf),
             dma((7,)),
             dma((2, HK, NB - 1)),
             dma((2, HK, NB - 1)),
@@ -549,10 +536,9 @@
             dma((2, 8)),
             dma((2, N_X, N_ZH)),
             dma((2, N_X, N_ZH)),
-            dma((4,)),
         ],
         compiler_params=pltpu.CompilerParams(
-            collective_id=0, has_side_effects=True, vmem_limit_bytes=60 * 1024 * 1024
+            collective_id=0, has_side_effects=True, vmem_limit_bytes=56 * 1024 * 1024
         ),
         cost_estimate=pl.CostEstimate(
             flops=2 * 6 * HQ * BLK * SPAN * HD,
@@ -566,13 +552,12 @@
     return pl.pallas_call(
         hand_over_kernel,
         out_shape=tuple(jax.ShapeDtypeStruct(part.shape, part.dtype) for part in results),
-        in_specs=[far] * 4,
+        in_specs=[near] * 4,
         out_specs=(far,) * 4,
-        scratch_shapes=[vmem(part.shape, part.dtype) for part in results]
-        + [dma((len(PIECES),)), dma((len(PIECES),))],
+        scratch_shapes=[dma((len(PIECES),))],
         compiler_params=pltpu.CompilerParams(vmem_limit_bytes=60 * 1024 * 1024),
         cost_estimate=pl.CostEstimate(flops=0, bytes_accessed=6 << 20, transcendentals=0),
-    )(*results)
+    )(*[pltpu.with_memory_space_constraint(part, pltpu.VMEM) for part in results])
 
 
 def solution(mesh):

time: 82.3 us -> 79.9 us (0.971)
  Pallas kernels: 81.5 us -> 79.1 us
    pallas_call x1, Pallas kernels: 78.8 us -> 77.5 us  [body(): pl.pallas_call(step_kernel, out_shape=(vmem(queries.shape, bf), vmem(quer...]
    pallas_call x1, Pallas kernels: 2.69 us -> 1.63 us  [body(): pl.pallas_call(hand_over_kernel, out_shape=tuple((jax.ShapeDtypeStruct(pa...]
where the time goes in v4:
time: 79.9 us; the launch traced here: 79.8 us
  Pallas kernels  79.1 us (99%)
    pallas_call x1, Pallas kernels, body(): pl.pallas_call(step_kernel, out_shape=(vmem(queries.shape, bf), vmem(quer...  77.5 us
    pallas_call x1, Pallas kernels, body(): pl.pallas_call(hand_over_kernel, out_shape=tuple((jax.ShapeDtypeStruct(pa...  1.63 us

profile of v4, /device:TPU:6, one launch (start us, length us, event | category | flops | bytes accessed | tf_op | source)
XLA Modules:
  0.0 79.8 jit_solution(13937599609843407228)
XLA Ops:
  0.6 77.5 %shard_map.111 = (bf16[128,4096]{1,0:T(8,128)(2,1)S(1)}, bf16[128,4096]{1,0:T(8,128)(2,1)S(1)}, bf16[128,512]{1,0:T(8,128)(2,1)S(1)}, bf16[512,512]{1,0:T(8,128)(2,1)S(1)}) custom-call(bf16[128,8192]{1,0:T(8,128)(2,1)} %x_ref.1, bf16[128,4096]{1,0:T(8,128)(2,1)} %q_hbm.1, bf16[128,512]{1,0:T(8,128)(2,1)} %k_hbm.1, bf16[128,512]{1,0:T(8,128)(2,1)} %v_hbm.1, ...), custom_call_target="tpu_custom_call" | custom-call | flops 4026531840 | bytes 8388608 | tf_op jit(solution)/shard_map/pallas_call | solution.py:488
  78.2 1.6 %shard_map.112 = (bf16[128,4096]{1,0:T(8,128)(2,1)}, bf16[128,4096]{1,0:T(8,128)(2,1)}, bf16[128,512]{1,0:T(8,128)(2,1)}, bf16[512,512]{1,0:T(8,128)(2,1)}) custom-call(bf16[128,4096]{1,0:T(8,128)(2,1)S(1)} %get-tuple-element.8.refs_0_, bf16[128,4096]{1,0:T(8,128)(2,1)S(1)} %get-tuple-element.9.refs_1_, bf16[128,512]{1,0:T(8,128)(2,1)S(1)} %get-tuple-element.10.refs_2_, ...), custom_call_target="tpu_custom_call" | custom-call | bytes 6291456 | tf_op jit(solution)/shard_map/pallas_call | solution.py:552

commit v5 on v4

--- a/solution.py
+++ b/solution.py
@@ -184,6 +184,16 @@
     def halo(which, g, by):
         src, span = ((k_hbm, k_span), (v_hbm, v_span))[which]
         slot = NB - 1 - by
+        if which == 1 and by < N_ZH:
+            first = (1 - (zh + by) // N_ZH) * ((NB - 1) * BLK)
+            return remote(
+                v_span.at[pl.ds(pl.multiple_of(first, BLK), BLK), lanes(g)],
+                v_span.at[pl.ds(slot * BLK, BLK), lanes(g)],
+                halo_s.at[which, g, by - 1],
+                halo_r.at[which, g, by - 1],
+                dp,
+                z_at(by),
+            )
         return remote(
             src.at[:, lanes(g)],
             span.at[pl.ds(slot * BLK, BLK), lanes(g)],
@@ -219,11 +229,23 @@
     def dk_back(g, by):
         return back(dk_part, dk_got, dk_s, dk_r, g, by)
 
-    def send_spans(which, first, last):
+    def send_keys_on():
+        @pl.loop(0, HK)
+        def _(g):
+            for by in range(1, NB):
+                halo(0, g, by).start()
+
+    def send_values_on():
+        @pl.loop(0, HK)
+        def _(g):
+            halo(1, g, NB - 1).start()
+
+    def spread_values(first, last):
         @pl.loop(first, last)
         def _(g):
-            for by in range(1, NB):
-                halo(which, g, by).start()
+            halo(1, g, NB - 1).wait_recv()
+            for by in range(1, N_ZH):
+                halo(1, g, by).start()
 
     def probs(first, last):
         @pl.loop(first, last)
@@ -244,7 +266,7 @@
     def grads(first, last, send=True):
         @pl.loop(first, last)
         def _(g):
-            for by in range(1, NB):
+            for by in range(1, N_ZH):
                 halo(1, g, by).wait_recv()
             dk = grads_of_group(
                 g, q_ref, k_span, v_span, go_ref, prob_ref, ds_ref, out_v, dq_v
@@ -396,7 +418,8 @@
             total = total + dk_got[by - 1].astype(f32)
         dk_v[...] = total.astype(bf)
 
-    send_spans(0, 0, HK)
+    send_keys_on()
+    send_values_on()
     for e in (4, 5, 2, 3, 6, 7, 1, 0):
         for j in range(2):
             x_share(e, j).start()
@@ -410,14 +433,15 @@
     gather_values(0)
     sum_values(1)
     gather_values(1)
-    send_spans(1, 0, 4)
+    spread_values(0, 4)
     turn_inputs()
     pass_values(0)
     partials(0)
     pass_values(1)
     partials(1)
-    grads(0, 3)
+    grads(0, 2)
     sum_x(0)
+    grads(2, 3)
     sum_x(1)
     grads(3, 4, False)
     adam(0)

time: 79.9 us -> 79 us (0.989)
  Pallas kernels: 79.1 us -> 77.5 us
    pallas_call x1, Pallas kernels: 77.5 us -> 75.8 us  [body(): pl.pallas_call(step_kernel, out_shape=(vmem(queries.shape, bf), vmem(quer...]
where the time goes in v5:
time: 79 us; the launch traced here: 78.1 us
  Pallas kernels  77.5 us (98%)
    pallas_call x1, Pallas kernels, body(): pl.pallas_call(step_kernel, out_shape=(vmem(queries.shape, bf), vmem(quer...  75.8 us
    pallas_call x1, Pallas kernels, body(): pl.pallas_call(hand_over_kernel, out_shape=tuple((jax.ShapeDtypeStruct(pa...  1.63 us

profile of v5, /device:TPU:6, one launch (start us, length us, event | category | flops | bytes accessed | tf_op | source)
XLA Modules:
  0.0 78.1 jit_solution(9687876404695189775)
XLA Ops:
  0.6 75.8 %shard_map.111 = (bf16[128,4096]{1,0:T(8,128)(2,1)S(1)}, bf16[128,4096]{1,0:T(8,128)(2,1)S(1)}, bf16[128,512]{1,0:T(8,128)(2,1)S(1)}, bf16[512,512]{1,0:T(8,128)(2,1)S(1)}) custom-call(bf16[128,8192]{1,0:T(8,128)(2,1)} %x_ref.1, bf16[128,4096]{1,0:T(8,128)(2,1)} %q_hbm.1, bf16[128,512]{1,0:T(8,128)(2,1)} %k_hbm.1, bf16[128,512]{1,0:T(8,128)(2,1)} %v_hbm.1, ...), custom_call_target="tpu_custom_call" | custom-call | flops 4026531840 | bytes 8388608 | tf_op jit(solution)/shard_map/pallas_call | solution.py:512
  76.5 1.6 %shard_map.112 = (bf16[128,4096]{1,0:T(8,128)(2,1)}, bf16[128,4096]{1,0:T(8,128)(2,1)}, bf16[128,512]{1,0:T(8,128)(2,1)}, bf16[512,512]{1,0:T(8,128)(2,1)}) custom-call(bf16[128,4096]{1,0:T(8,128)(2,1)S(1)} %get-tuple-element.8.refs_0_, bf16[128,4096]{1,0:T(8,128)(2,1)S(1)} %get-tuple-element.9.refs_1_, bf16[128,512]{1,0:T(8,128)(2,1)S(1)} %get-tuple-element.10.refs_2_, ...), custom_call_target="tpu_custom_call" | custom-call | bytes 6291456 | tf_op jit(solution)/shard_map/pallas_call | solution.py:576

commit v6 on v5

--- a/solution.py
+++ b/solution.py
@@ -129,7 +129,7 @@
     out_v, dq_v, dk_v, up_v,
     q_ref, go_ref, seg_ref, m_ref, s_ref,
     bias_ref, prob_ref, ds_ref, k_span, v_span, dv_part, dk_part, dv_got, dk_got,
-    xs_ref, xt_ref, vg_ref, sx_ref, rx_ref, acc_ref, sz_ref, rz_ref,
+    xs_ref, xt_ref, vg_ref, part_ref, sx_ref, rx_ref, acc_ref, sz_ref, rz_ref,
     load_l, halo_s, halo_r, x_s, x_r, x_l, dv_s, dv_r, dk_s, dk_r, vg_s, vg_r,
     rx_s, rx_r, rz_s, rz_r, ag_s, ag_r,
 ):
@@ -176,6 +176,7 @@
     partners = [(dp, ctx_at(by)) for by in (1, 2, 3, 4, -1, -2, -3, -4, 8)]
     partners += [(share_at(e // 2, e % 2), me) for e in range(1, 8)]
     partners += [(zl_at(1), z_at(dh)) for dh in range(N_ZH)]
+    partners += [(share_at(0, 1), x_at(dx)) for dx in range(1, N_X)]
     barrier = pltpu.get_barrier_semaphore()
     for partner in partners:
         pl.semaphore_signal(barrier, inc=1, device_id=partner, device_id_type=MESH)
@@ -203,14 +204,26 @@
             ctx_at(by),
         )
 
-    def x_share(e, j):
-        dy, dc = e // 2, e % 2
-        first = (((y + dy) % N_Y) * 4 + j * 2 + (core + dc) % 2) * 512
-        src = x_ref.at[:, pl.ds(pl.multiple_of(first, 512), 512)]
-        dst = xs_ref.at[e, :, pl.ds(j * 512, 512)]
+    def peer_at(p, by, dc):
+        if p == 0:
+            return share_at(by, dc), me
+        return share_at(0, dc), x_at(by)
+
+    def x_share(p, e, n):
+        by, dc = e // 2, e % 2
+        other = (core + dc) % 2
+        if p == 0:
+            first, size = ((y + by) % N_Y * 4 + other) * 512, 512
+        else:
+            first, size = (n * 4 + 2 + other) * 512 + (x + by) % N_X * 128, 128
+        src = x_ref.at[:, pl.ds(pl.multiple_of(first, size), size)]
+        dst = xs_ref.at[p, e, :, pl.ds(n * size, size)]
         if e == 0:
-            return pltpu.make_async_copy(src, dst, x_l.at[j])
-        return remote(src, dst, x_s.at[e, j], x_r.at[e, j], share_at(dy, dc), me)
+            return pltpu.make_async_copy(src, dst, x_l.at[p, n])
+        return remote(src, dst, x_s.at[p, e, n], x_r.at[p, e, n], *peer_at(p, by, dc))
+
+    SHARES = [(0, e, 0) for e in (4, 5, 2, 3, 6, 7, 1, 0)]
+    SHARES += [(1, e, n) for e in (4, 5, 2, 3, 6, 7, 1, 0) for n in range(N_Y)]
 
     def back(part, got, send, recv, g, by):
         slot = NB - 1 - by
@@ -286,66 +299,84 @@
         total = dv_part[own_rows, columns(h)].astype(f32)
         for by in range(1, NB):
             total = total + dv_got[by - 1, :, columns(h)].astype(f32)
-        vg_ref[h, 0] = total.astype(bf)
-
-    def vg_send(h, dy):
-        e = 2 * dy
-        return remote(
-            vg_ref.at[h, 0], vg_ref.at[h, e], vg_s.at[h, e], vg_r.at[h, e], share_at(dy, 0), me
-        )
-
-    def vg_pass(h, dy):
-        e = 2 * dy
-        return remote(
-            vg_ref.at[h, e],
-            vg_ref.at[h, e + 1],
-            vg_s.at[h, e + 1],
-            vg_r.at[h, e + 1],
-            share_at(0, 1),
-            me,
+        vg_ref[0, h, 0] = total.astype(bf)
+        vg_ref[1, h, 0] = total.astype(bf)
+
+    def vg_send(p, h, by):
+        e = 2 * by
+        return remote(
+            vg_ref.at[p, h, 0],
+            vg_ref.at[p, h, e],
+            vg_s.at[p, h, e],
+            vg_r.at[p, h, e],
+            *peer_at(p, by, 0),
+        )
+
+    def vg_pass(p, h, by):
+        e = 2 * by
+        return remote(
+            vg_ref.at[p, h, e],
+            vg_ref.at[p, h, e + 1],
+            vg_s.at[p, h, e + 1],
+            vg_r.at[p, h, e + 1],
+            *peer_at(p, 0, 1),
         )
 
     def gather_values(h):
-        for dy in (2, 1, 3):
-            vg_send(h, dy).start()
-        vg_pass(h, 0).start()
+        for by in (2, 1, 3):
+            for p in range(2):
+                vg_send(p, h, by).start()
+        for p in range(2):
+            vg_pass(p, h, 0).start()
 
     def pass_values(h):
-        for dy in (1, 3, 2):
-            vg_send(h, dy).wait_recv()
-            vg_pass(h, dy).start()
-
-    def turn_inputs():
-        for e in range(8):
-            for j in range(2):
-                if e == 0:
-                    x_share(e, j).wait()
-                else:
-                    x_share(e, j).wait_recv()
+        for by in (1, 3, 2):
+            for p in range(2):
+                vg_send(p, h, by).wait_recv()
+                vg_pass(p, h, by).start()
+
+    def send_inputs(which):
+        for share in SHARES:
+            if share[0] == which:
+                x_share(*share).start()
+
+    def turn_inputs(which):
+        for p, e, n in SHARES:
+            if p != which:
+                continue
+            if e == 0:
+                x_share(p, e, n).wait()
+            else:
+                x_share(p, e, n).wait_recv()
 
         @pl.loop(0, 8)
         def _(e):
-            xt_ref[:, lanes(e)] = xs_ref[e].T
-
-    def x_piece(h, d):
-        return remote(
-            sx_ref.at[h, d], rx_ref.at[h, d], rx_s.at[h, d], rx_r.at[h, d], dp, x_at(d)
-        )
-
-    def partial_for(h, d):
-        first = ((x + d) % N_X) * 128
-        left = jnp.concatenate(
-            [xt_ref[pl.ds(pl.multiple_of(j * 512 + first, 128), 128), :] for j in range(2)], axis=0
-        )
-        return jnp.dot(left, vg_ref[h].reshape(8 * BLK, HALF), preferred_element_type=f32)
+            xt_ref[which, :, lanes(e)] = xs_ref[which, e].T
+
+    def piece_rows(p, d):
+        place = (x + d) % N_X if p == 0 else (y + d) % N_Y
+        return pl.ds(pl.multiple_of(place * 128, 128), 128)
+
+    def x_piece(p, h, d):
+        return remote(
+            sx_ref.at[p, h, piece_rows(p, d), :],
+            rx_ref.at[p, h, d],
+            rx_s.at[p, h, d],
+            rx_r.at[p, h, d],
+            *((dp, x_at(d)) if p == 0 else (share_at(d, 0), me)),
+        )
 
     def partials(h):
-        for dy in range(N_Y):
-            vg_pass(h, dy).wait_recv()
-        for d in (2, 1, 3):
-            sx_ref[h, d] = partial_for(h, d).astype(bf)
-            x_piece(h, d).start()
-        acc_ref[h] = partial_for(h, 0)
+        for p in range(2):
+            for by in range(N_Y):
+                vg_pass(p, h, by).wait_recv()
+            partial = jnp.dot(
+                xt_ref[p], vg_ref[p, h].reshape(8 * BLK, HALF), preferred_element_type=f32
+            )
+            part_ref[p, h] = partial
+            sx_ref[p, h] = partial.astype(bf)
+            for d in (2, 1, 3):
+                x_piece(p, h, d).start()
 
     def z_rows(dl, dh):
         first = ((zl + dl) % 2) * 128 + ((zh + dh) % N_ZH) * ROWS
@@ -363,13 +394,14 @@
         )
 
     def sum_x(h):
-        for d in (1, 3, 2):
-            x_piece(h, d).wait_recv()
-        total = acc_ref[h]
-        for d in range(1, N_X):
-            total = total + rx_ref[h, d].astype(f32)
-        acc_ref[h] = total
-        sz_ref[h] = total.astype(bf)
+        for p in range(2):
+            for d in (1, 3, 2):
+                x_piece(p, h, d).wait_recv()
+            total = part_ref[p, h, piece_rows(p, 0), :]
+            for d in range(1, N_X):
+                total = total + rx_ref[p, h, d].astype(f32)
+            acc_ref[h, p * 128 : (p + 1) * 128, :] = total
+            sz_ref[h, p * 128 : (p + 1) * 128, :] = total.astype(bf)
         for e in (4, 5, 3, 2, 6, 7, 1):
             z_piece(h, e).start()
 
@@ -420,21 +452,21 @@
 
     send_keys_on()
     send_values_on()
-    for e in (4, 5, 2, 3, 6, 7, 1, 0):
-        for j in range(2):
-            x_share(e, j).start()
     loads[0].wait()
     build_bias(me, N_CTX, seg_ref, bias_ref)
     for load in loads[1:]:
         load.wait()
 
+    send_inputs(0)
+    send_inputs(1)
     probs(0, 4)
     sum_values(0)
     gather_values(0)
     sum_values(1)
     gather_values(1)
     spread_values(0, 4)
-    turn_inputs()
+    turn_inputs(0)
+    turn_inputs(1)
     pass_values(0)
     partials(0)
     pass_values(1)
@@ -463,16 +495,17 @@
             dv_back(g, by).wait_send()
             dk_back(g, by).wait_send()
 
-    for e in range(1, 8):
-        for j in range(2):
-            x_share(e, j).wait_send()
+    for p, e, n in SHARES:
+        if e:
+            x_share(p, e, n).wait_send()
     for h in range(2):
-        for dy in range(1, N_Y):
-            vg_send(h, dy).wait_send()
-        for dy in range(N_Y):
-            vg_pass(h, dy).wait_send()
-        for d in range(1, N_X):
-            x_piece(h, d).wait_send()
+        for p in range(2):
+            for by in range(1, N_Y):
+                vg_send(p, h, by).wait_send()
+            for by in range(N_Y):
+                vg_pass(p, h, by).wait_send()
+            for d in range(1, N_X):
+                x_piece(p, h, d).wait_send()
         for e in range(1, 8):
             z_piece(h, e).wait_send()
         for dh in range(1, N_ZH):
@@ -534,28 +567,29 @@
             vmem((SPAN, WIDTH), bf),
             vmem((NB - 1, BLK, WIDTH), bf),
             vmem((NB - 1, BLK, WIDTH), bf),
-            vmem((8, BLK, 1024), bf),
-            vmem((1024, 8 * BLK), bf),
-            vmem((2, 8, BLK, HALF), bf),
-            vmem((2, N_X, 256, HALF), bf),
-            vmem((2, N_X, 256, HALF), bf),
+            vmem((2, 8, BLK, 512), bf),
+            vmem((2, 512, 8 * BLK), bf),
+            vmem((2, 2, 8, BLK, HALF), bf),
+            vmem((2, 2, 512, HALF), f32),
+            vmem((2, 2, 512, HALF), bf),
+            vmem((2, 2, N_X, 128, HALF), bf),
             vmem((2, 256, HALF), f32),
             vmem((2, 256, HALF), bf),
             vmem((2, 8, ROWS, HALF), bf),
             dma((7,)),
             dma((2, HK, NB - 1)),
             dma((2, HK, NB - 1)),
-            dma((8, 2)),
-            dma((8, 2)),
-            dma((2,)),
+            dma((2, 8, N_Y)),
+            dma((2, 8, N_Y)),
+            dma((2, N_Y)),
             dma((HK, NB - 1)),
             dma((HK, NB - 1)),
             dma((HK, NB - 1)),
             dma((HK, NB - 1)),
-            dma((2, 8)),
-            dma((2, 8)),
-            dma((2, N_X)),
-            dma((2, N_X)),
+            dma((2, 2, 8)),
+            dma((2, 2, 8)),
+            dma((2, 2, N_X)),
+            dma((2, 2, N_X)),
             dma((2, 8)),
             dma((2, 8)),
             dma((2, N_X, N_ZH)),

time: 79 us -> 81.7 us (1.034)
  the two profiles are of different devices: /device:TPU:6 before, /device:TPU:16 now
where the time goes in v6:
time: 81.7 us; the launch traced here: 81.6 us
  Pallas kernels  81 us (99%)
    pallas_call x1, Pallas kernels, body(): pl.pallas_call(step_kernel, out_shape=(vmem(queries.shape, bf), vmem(quer...  79.4 us

profile of v6, /device:TPU:16, one launch (start us, length us, event | category | flops | bytes accessed | tf_op | source)
XLA Modules:
  0.0 81.6 jit_solution(9206968125940563907)
XLA Ops:
  0.6 79.4 %shard_map.111 = (bf16[128,4096]{1,0:T(8,128)(2,1)S(1)}, bf16[128,4096]{1,0:T(8,128)(2,1)S(1)}, bf16[128,512]{1,0:T(8,128)(2,1)S(1)}, bf16[512,512]{1,0:T(8,128)(2,1)S(1)}) custom-call(bf16[128,8192]{1,0:T(8,128)(2,1)} %x_ref.1, bf16[128,4096]{1,0:T(8,128)(2,1)} %q_hbm.1, bf16[128,512]{1,0:T(8,128)(2,1)} %k_hbm.1, bf16[128,512]{1,0:T(8,128)(2,1)} %v_hbm.1, ...), custom_call_target="tpu_custom_call" | custom-call | flops 4026531840 | bytes 8388608 | tf_op jit(solution)/shard_map/pallas_call | solution.py:545
  80.0 1.6 %shard_map.112 = (bf16[128,4096]{1,0:T(8,128)(2,1)}, bf16[128,4096]{1,0:T(8,128)(2,1)}, bf16[128,512]{1,0:T(8,128)(2,1)}, bf16[512,512]{1,0:T(8,128)(2,1)}) custom-call(bf16[128,4096]{1,0:T(8,128)(2,1)S(1)} %get-tuple-element.8.refs_0_, bf16[128,4096]{1,0:T(8,128)(2,1)S(1)} %get-tuple-element.9.refs_1_, bf16[128,512]{1,0:T(8,128)(2,1)S(1)} %get-tuple-element.10.refs_2_, ...), custom_call_target="tpu_custom_call" | custom-call | bytes 6291456 | tf_op jit(solution)/shard_map/pallas_call | solution.py:610
